TPU v7x, 32 devices: a whole 2x2x4 slice. The times are simulated.
32 devices in a mesh: dp: 4 (over z), tensor: 8 (over y, x, core).
Axes of the slice: x: 2, y: 2, z: 4, core: 2. Of those that a mesh axis runs over, the one named last changes fastest.
Arguments:
- pages: bfloat16 [2, 16, 64, 2048], P(None, 'dp', None, 'tensor'), may hold values from -8 to 8
- page_table: int32 [4, 2], replicated, may hold values from 0 to 15, as said below
- page_count: int32 [4], replicated, may hold values from 1 to 2
- last_len: int32 [4], replicated, may hold values from 1 to 64
- targets: int32 [4, 128], P('dp'), may hold values from 0 to 65535
- mix_key: float32 [2, 2048], P(None, 'tensor'), may hold values from 0.05 to 0.95
- w_key: bfloat16 [2, 2048, 8192], P(None, None, 'tensor'), may hold values from -0.125 to 0.125
- w_value: bfloat16 [2, 8192, 2048], P(None, 'tensor'), may hold values from -0.0625 to 0.0625
- ln_gain: float32 [2, 2048], replicated, may hold values from 0.5 to 1.5
- ln_bias: float32 [2, 2048], replicated, may hold values from -2 to 2
- head: bfloat16 [2, 2048, 65536], P(None, 'dp', 'tensor'), may hold values from -8 to 8
Outputs:
- token_logprob: float32 [4, 128], P('dp', 'tensor')
- ratio_sum: float32 [4], P('dp')
Inputs may be any that keep to these rules, and one draw needn't show every extreme that they name: Entries are distinct; the page lives on dp device page_table[r, p] // 4.
All inputs are finite; a program needn't handle non-finite values.
Results may differ from a plain program's by a relative error of at most 0.0029.
The roundings to bfloat16 on the way count: a program that leaves them out, or rounds other values in their place, can miss the bound.
Values may be sent and summed in bfloat16 or wider, within the bound.
No kernel may reach another device: no remote copies, remote signals or barrier semaphores. Data moves between devices by JAX's collectives and lax.ppermute only.
A program may use at most 192 MiB of HBM per device.

v0:
```python
import jax
import jax.numpy as jnp
from jax import lax
from jax.sharding import PartitionSpec as P

D = 2048


epsilon = 1e-05


def joined(value, axis, join):
    pieces = jax.tree.map(lambda part: lax.all_gather(part, axis), value)
    head = jax.tree.map(lambda part: part[0], pieces)
    tail = jax.tree.map(lambda part: part[1:], pieces)
    total, _ = lax.scan(lambda total, piece: (join(total, piece), None), head, tail)
    return total


def combine(left_stats, right_stats):
    peak = jnp.maximum(left_stats[0], right_stats[0])
    totals = left_stats[1] * jnp.exp(left_stats[0] - peak) + right_stats[1] * jnp.exp(
        right_stats[0] - peak
    )
    return (peak, totals, left_stats[2] + right_stats[2])


def body(
    pages,
    page_table,
    page_count,
    last_len,
    targets,
    mix_key,
    w_key,
    w_value,
    ln_gain,
    ln_bias,
    head,
):
    tensor_count = lax.axis_size("tensor")
    owner = lax.axis_index("dp")
    tensor_index = lax.axis_index("tensor")
    page_len = pages.shape[2]
    width_local = pages.shape[3]
    page_cap = page_table.shape[1]
    slot_count = page_cap * page_len
    live_pages = jnp.arange(page_cap)[None, :] < page_count[:, None]
    table_row = page_table[owner]
    everything = lax.all_gather(pages, "dp", axis=1, tiled=True)
    states = jnp.take(everything, table_row, axis=1)
    states = jnp.where(live_pages[owner][None, :, None, None], states, jnp.zeros_like(states))
    states = states.reshape(2, slot_count, width_local)
    state_f = states.astype(jnp.float32)
    previous = jnp.concatenate(
        [jnp.zeros((2, 1, width_local), jnp.float32), state_f[:, :-1]], axis=1
    )
    shifted = (state_f + (previous - state_f) * mix_key[:, None, :]).astype(jnp.bfloat16)
    hidden = jnp.einsum(
        "msd,mdf->msf",
        lax.all_gather(shifted, "tensor", axis=2, tiled=True),
        w_key,
        preferred_element_type=jnp.float32,
    )
    key_act = (jnp.maximum(hidden, 0.0) ** 2).astype(jnp.bfloat16)
    partial_out = jnp.einsum("msf,mfd->msd", key_act, w_value, preferred_element_type=jnp.float32)
    ffn_out = lax.psum_scatter(partial_out, "tensor", scatter_dimension=2, tiled=True)
    residual = state_f + ffn_out
    row_sum, row_square = lax.psum(
        (jnp.sum(residual, axis=-1), jnp.sum(residual * residual, axis=-1)), "tensor"
    )
    average = row_sum / D
    variance = row_square / D - average * average
    gain_local = lax.dynamic_slice_in_dim(ln_gain, tensor_index * width_local, width_local, 1)
    bias_local = lax.dynamic_slice_in_dim(ln_bias, tensor_index * width_local, width_local, 1)
    normed_local = (
        (residual - average[..., None])
        * lax.rsqrt(variance + epsilon)[..., None]
        * gain_local[:, None, :]
        + bias_local[:, None, :]
    ).astype(jnp.bfloat16)
    normed = lax.all_gather(normed_local, "tensor", axis=2, tiled=True)
    vocab_local = head.shape[2]
    logits = jnp.einsum(
        "msd,mdv->msv",
        normed,
        lax.all_gather(head, "dp", axis=1, tiled=True),
        preferred_element_type=jnp.float32,
    )
    peak = jnp.max(logits, axis=-1)
    totals = jnp.sum(jnp.exp(logits - peak[..., None]), axis=-1)
    vocab_ids = jnp.arange(vocab_local) + tensor_index * vocab_local
    matches = vocab_ids[None, None, :] == targets[0][None, :, None]
    target_logit = jnp.sum(jnp.where(matches, logits, 0.0), axis=-1)
    peak, totals, target_logit = joined((peak, totals, target_logit), "tensor", combine)
    logp = target_logit - peak - jnp.log(totals)
    length = (page_count[owner] - 1) * page_len + last_len[owner]
    valid = jnp.arange(slot_count) < length
    policy_row = jnp.where(valid, logp[0], 0.0)
    ratio = jnp.sum(jnp.where(valid, logp[0] - logp[1], 0.0))
    share = slot_count // tensor_count
    token_part = lax.dynamic_slice_in_dim(policy_row, tensor_index * share, share)[None, :]
    return (token_part, ratio[None])


def solution(mesh):
    placed = (
        P(None, "dp", None, "tensor"),
        P(),
        P(),
        P(),
        P("dp", None),
        P(None, "tensor"),
        P(None, None, "tensor"),
        P(None, "tensor", None),
        P(),
        P(),
        P(None, "dp", "tensor"),
    )
    return jax.shard_map(
        body, mesh=mesh, in_specs=placed, out_specs=(P("dp", "tensor"), P("dp")), check_vma=False
    )
```

profile of v0, /device:TPU:1, one launch (start us, length us, event | category | flops | bytes accessed | tf_op | source)
XLA Modules:
  0.0 1335.7 jit_solution(6964521749321124661)
XLA Ops:
  7.2 0.0 copy-start
  7.2 0.0 all-gather.11.cloned.1.call-start
  7.2 0.7 all-gather.11.cloned.1.call-update
  7.9 0.0 all-gather.13.cloned.1.call-start
  8.0 0.0 copy-done
  8.0 0.2 dynamic-slice_reduce_fusion
  8.2 0.1 broadcast_in_dim.68
  8.3 0.1 broadcast_in_dim.69
  8.3 0.7 iota_compare_fusion
  9.1 0.1 broadcast_in_dim.65
  9.2 0.1 broadcast_in_dim.66
  9.3 30.2 %all-gather.11.cloned.1.call-done = bf16[2,16,64,256]{3,2,1,0:T(8,128)(2,1)} async-done(((bf16[2,4,64,256]{3,2,1,0:T(8,128)(2,1)}), bf16[2,16,64,256]{3,2,1,0:T(8,128)(2,1)}) %all-gather.11.cloned.1.call-update) | async-done | bytes 1048592 | tf_op jit(solution)/shard_map/all_gather | solution.py:50
  39.5 1.8 gather_fusion
  41.3 0.1 fusion.7
  41.4 1.5 add_convert_fusion.1
  42.9 0.0 all-gather.13.cloned.1.call-update
  42.9 0.0 reduce-scatter.2.cloned.1.call-start
  43.0 23.7 %all-gather.13.cloned.1.call-done = bf16[2,128,2048]{2,1,0:T(8,128)(2,1)} async-done(((bf16[2,128,256]{2,1,0:T(8,128)(2,1)}), bf16[2,128,2048]{2,1,0:T(8,128)(2,1)}) %all-gather.13.cloned.1.call-update) | async-done | bytes 1048592 | tf_op jit(solution)/shard_map/all_gather | solution.py:61
  66.7 9.8 fusion.4
  76.5 0.0 reduce-scatter.2.cloned.1.call-update
  76.5 0.0 all-gather.15.cloned.1.call-start
  76.5 0.7 constant_dynamic-slice_fusion.1
  77.2 40.2 %reduce-scatter.2.cloned.1.call-done = f32[2,128,256]{2,1,0:T(8,128)} async-done(((f32[2,128,2048]{2,1,0:T(8,128)}), f32[2,128,256]{2,1,0:T(8,128)}) %reduce-scatter.2.cloned.1.call-update) | async-done | bytes 262160 | tf_op jit(solution)/shard_map/reduce_scatter | solution.py:67
  117.4 1.2 fusion.12
  118.6 11.9 all-reduce.1
  130.5 1.8 add_convert_fusion
  132.3 0.0 all-gather.15.cloned.1.call-update
  132.3 0.0 copy-start.2
  132.3 0.0 copy-start.3
  132.3 0.0 copy-start.1
  132.3 0.0 all-gather.17.cloned.1.call-start
  132.4 0.5 all-gather.17.cloned.1.call-update
  132.9 0.0 copy-done.2
  132.9 0.6 dynamic_slice.31
  133.5 0.0 copy-done.3
  133.5 0.6 dynamic_slice.32
  135.3 0.0 copy-done.1
  135.3 0.6 broadcast_compare_fusion
  135.9 21.3 %all-gather.15.cloned.1.call-done = bf16[2,128,2048]{2,1,0:T(8,128)(2,1)} async-done(((bf16[2,128,256]{2,1,0:T(8,128)(2,1)}), bf16[2,128,2048]{2,1,0:T(8,128)(2,1)}) %all-gather.15.cloned.1.call-update) | async-done | bytes 1048592 | tf_op jit(solution)/shard_map/all_gather | solution.py:82
  157.2 1112.0 %all-gather.17.cloned.1.call-done = bf16[2,2048,8192]{2,1,0:T(8,128)(2,1)} async-done(((bf16[2,512,8192]{2,1,0:T(8,128)(2,1)}), bf16[2,2048,8192]{2,1,0:T(8,128)(2,1)}) %all-gather.17.cloned.1.call-update) | async-done | bytes 67108880 | tf_op jit(solution)/shard_map/all_gather | solution.py:87
  1269.2 27.4 %fusion.13 = (f32[2,128]{1,0:T(2,128)S(1)}, f32[2,128,8192]{2,1,0:T(8,128)}) fusion(bf16[2,128,2048]{2,1,0:T(8,128)(2,1)} %all-gather.15.cloned.1.call-done, bf16[2,2048,8192]{2,1,0:T(8,128)(2,1)} %all-gather.17.cloned.1.call-done), kind=kOutput, calls=%fused_computation.47 | convolution fusion | flops 8592031744 | bytes 76547072 | tf_op jit(solution)/shard_map/msd,mdv->msv/dot_general | solution.py:84
  1296.6 5.1 select_reduce_fusion
  1301.7 9.1 all-gather.5
  1310.9 8.8 all-gather.4
  1319.7 7.9 all-gather.3
  1327.6 0.3 while.14
  1327.9 0.6 fusion.8
  1328.5 0.6 dynamic-slice_bitcast_fusion.1
  (21 shorter events, 0.3 us)
Async XLA Ops:
  7.2 0.8 copy-start
  7.2 32.3 %all-gather.11.cloned.1.call-start = ((), (), s32[]{:S(2)}) async-start(), calls=%async_computation.1 | async-start | bytes 1310720 | tf_op jit(solution)/shard_map/all_gather | solution.py:50
  7.9 58.8 %all-gather.13.cloned.1.call-start = ((), (), s32[]{:S(2)}) async-start(), calls=%async_computation.2 | async-start | bytes 1179648 | tf_op jit(solution)/shard_map/all_gather | solution.py:61
  42.9 74.5 %reduce-scatter.2.cloned.1.call-start = ((), (), s32[]{:S(2)}) async-start(), calls=%async_computation.3 | async-start | bytes 2359296 | tf_op jit(solution)/shard_map/reduce_scatter | solution.py:67
  76.5 80.7 %all-gather.15.cloned.1.call-start = ((), (), s32[]{:S(2)}) async-start(), calls=%async_computation.4 | async-start | bytes 1179648 | tf_op jit(solution)/shard_map/all_gather | solution.py:82
  132.3 0.7 copy-start.2
  132.3 1.2 copy-start.3
  132.3 3.0 copy-start.1
  132.3 1136.9 %all-gather.17.cloned.1.call-start = ((), (), s32[]{:S(2)}) async-start(), calls=%async_computation.5 | async-start | bytes 83886080 | tf_op jit(solution)/shard_map/all_gather | solution.py:87
Sparse Core Ops, SparseCore 0:
  9.6 29.8 all-gather.10
  43.0 23.6 all-gather.12
  76.6 40.7 reduce-scatter.1
  132.4 24.7 all-gather.14
  158.7 1110.4 all-gather.16
where the time goes:
time: 1340 us
  waiting for transfers between devices  1230 us (92%)
  blocking collectives  37.7 us (3%)
  matrix products  37.2 us (3%)
  between operations  15.1 us (1%)
    all_gather x1, waiting for transfers between devices, body(): lax.all_gather(head, 'dp', axis=1, tiled=True)  1110 us
    reduce_scatter x1, waiting for transfers between devices, body(): lax.psum_scatter(partial_out, 'tensor', scatter_dimension=2, tiled=True)  40.2 us
    all_gather x1, waiting for transfers between devices, body(): everything = lax.all_gather(pages, 'dp', axis=1, tiled=True)  30.2 us
    dot_general x1, matrix products, body(): jnp.einsum('msd,mdv->msv', normed, lax.all_gather(head, 'dp', axis=1, til...  27.4 us
  transfers between devices with their start and end apart: 5, of which 5 were waited for; matrix products, arithmetic and copies ran while one was open for 0% of the time, Pallas kernels for 0%

commit v1 on v0

v1 whole, which is shorter than its diff:
```python
import jax
import jax.numpy as jnp
from jax import lax
from jax.sharding import PartitionSpec as P

epsilon = 1e-05


def swap(value, axis, mask):
    count = lax.axis_size(axis)
    return lax.ppermute(value, axis, [(i, i ^ mask) for i in range(count)])


def ordered(pieces, index):
    pieces = list(pieces)
    bit = 1
    while bit < len(pieces):
        flip = (index & bit) != 0
        pieces = [jnp.where(flip, pieces[k ^ bit], pieces[k]) for k in range(len(pieces))]
        bit *= 2
    return pieces


def gather_chips(value):
    count = lax.axis_size("tensor")
    far = [value] + [swap(value, "tensor", k) for k in range(2, count, 2)]
    pieces = []
    for piece in far:
        pieces += [piece, swap(piece, "tensor", 1)]
    return pieces


def spread(value, axis):
    return [value] + [swap(value, axis, k) for k in range(1, lax.axis_size(axis))]


def body(
    pages,
    page_table,
    page_count,
    last_len,
    targets,
    mix_key,
    w_key,
    w_value,
    ln_gain,
    ln_bias,
    head,
):
    tensor_count = lax.axis_size("tensor")
    layer_count = lax.axis_size("dp")
    layer = lax.axis_index("dp")
    place = lax.axis_index("tensor")
    models, rows_held, page_len, width_local = pages.shape
    width = ln_gain.shape[1]
    page_cap = page_table.shape[1]
    slot_count = page_cap * page_len
    share = slot_count // tensor_count
    depth = head.shape[1]
    vocab_held = head.shape[2]
    vocab_part = vocab_held // layer_count

    states = None
    own_rows = page_table[layer]
    for k in range(layer_count):
        wanted = page_table[layer ^ k]
        block = jnp.take(pages, wanted % rows_held, axis=1)
        got = block if k == 0 else swap(block, "dp", k)
        here = (own_rows // rows_held) == (layer ^ k)
        here = jnp.logical_and(here, jnp.arange(page_cap) < page_count[layer])
        got = jnp.where(here[None, :, None, None], got, jnp.zeros_like(got))
        states = got if states is None else states + got

    head, _ = lax.optimization_barrier((head, states))
    head_parts = []
    for k in range(layer_count):
        part = lax.dynamic_slice_in_dim(head, (layer ^ k) * vocab_part, vocab_part, 2)
        head_parts.append(part if k == 0 else swap(part, "dp", k))

    states = states.reshape(models, slot_count, width_local)
    state_f = states.astype(jnp.float32)
    previous = jnp.concatenate(
        [jnp.zeros((models, 1, width_local), jnp.float32), state_f[:, :-1]], axis=1
    )
    shifted = (state_f + (previous - state_f) * mix_key[:, None, :]).astype(jnp.bfloat16)
    shifted = jnp.concatenate(ordered(gather_chips(shifted), place), axis=2)
    hidden = jnp.einsum("msd,mdf->msf", shifted, w_key, preferred_element_type=jnp.float32)
    key_act = (jnp.maximum(hidden, 0.0) ** 2).astype(jnp.bfloat16)
    mixed = jnp.einsum("msf,mfd->msd", key_act, w_value, preferred_element_type=jnp.float32)
    mine = (jnp.arange(tensor_count) == place)[None, None, :, None]
    mixed = mixed.reshape(models, slot_count, tensor_count, width_local)
    mixed = (mixed + jnp.where(mine, state_f[:, :, None, :], 0.0)).reshape(
        models, slot_count, width
    )

    half = jnp.stack([mixed[:, k * share : (k + 1) * share] for k in range(tensor_count)])
    half = half.reshape((tensor_count // 2, 2) + half.shape[1:])
    core = place % 2
    keep = lax.dynamic_index_in_dim(half, core, 1, False)
    give = lax.dynamic_index_in_dim(half, 1 - core, 1, False)
    keep = keep + swap(give, "tensor", 1)
    chip = place // 2
    residual = lax.dynamic_index_in_dim(keep, chip, 0, False)
    for k in range(1, tensor_count // 2):
        residual = residual + swap(
            lax.dynamic_index_in_dim(keep, chip ^ k, 0, False), "tensor", 2 * k
        )

    average = jnp.sum(residual, axis=-1) / width
    variance = jnp.sum(residual * residual, axis=-1) / width - average * average
    normed = (
        (residual - average[..., None]) * lax.rsqrt(variance + epsilon)[..., None]
    ) * ln_gain[:, None, :] + ln_bias[:, None, :]
    normed = normed.astype(jnp.bfloat16)

    column = jnp.stack(ordered(spread(normed, "dp"), layer), axis=1)
    everything = jnp.stack(ordered(gather_chips(column), place), axis=2)
    everything = everything.reshape(models, layer_count * slot_count, width)

    logits = None
    for k in range(layer_count):
        features = lax.dynamic_slice_in_dim(everything, (layer ^ k) * depth, depth, 2)
        term = jnp.einsum(
            "msd,mdv->msv", features, head_parts[k], preferred_element_type=jnp.float32
        )
        logits = term if logits is None else logits + term

    wanted = jnp.concatenate(ordered(spread(targets, "dp"), layer), axis=0).reshape(-1)
    first = place * vocab_held + layer * vocab_part
    matches = (jnp.arange(vocab_part) + first)[None, None, :] == wanted[None, :, None]
    peak = jnp.max(logits, axis=-1)
    totals = jnp.sum(jnp.exp(logits - peak[..., None]), axis=-1)
    target_logit = jnp.sum(jnp.where(matches, logits, 0.0), axis=-1)
    stats = jnp.stack([peak, totals, target_logit])

    stats = stats.reshape(3, models, layer_count, slot_count)
    mine = []
    for k in range(layer_count):
        part = lax.dynamic_index_in_dim(stats, layer ^ k, 2, False)
        mine.append(part if k == 0 else swap(part, "dp", k))
    mine = jnp.concatenate(ordered(gather_chips(jnp.stack(ordered(mine, layer))), place))
    top = jnp.max(mine[:, 0], axis=0)
    totals = jnp.sum(mine[:, 1] * jnp.exp(mine[:, 0] - top), axis=0)
    logp = jnp.sum(mine[:, 2], axis=0) - top - jnp.log(totals)

    length = (page_count[layer] - 1) * page_len + last_len[layer]
    valid = jnp.arange(slot_count) < length
    policy_row = jnp.where(valid, logp[0], 0.0)
    ratio = jnp.sum(jnp.where(valid, logp[0] - logp[1], 0.0))
    token_part = lax.dynamic_slice_in_dim(policy_row, place * share, share)[None, :]
    return (token_part, ratio[None])


def solution(mesh):
    placed = (
        P(None, "dp", None, "tensor"),
        P(),
        P(),
        P(),
        P("dp", None),
        P(None, "tensor"),
        P(None, None, "tensor"),
        P(None, "tensor", None),
        P(),
        P(),
        P(None, "dp", "tensor"),
    )
    return jax.shard_map(
        body, mesh=mesh, in_specs=placed, out_specs=(P("dp", "tensor"), P("dp")), check_vma=False
    )
```

time: 1340 us -> 520 us (0.39)
  waiting for transfers between devices: 1230 us -> 383 us
  starting transfers between devices: 0.2 us -> 58.3 us
  blocking collectives: 37.7 us -> 0 us
    all_gather x4 -> x0, waiting for transfers between devices: 1190 us -> none  [the longest x1 1110 us: body(): lax.all_gather(head, 'dp', axis=1, tiled=True)]
    ppermute x0 -> x40, waiting for transfers between devices: none -> 383 us  [swap(): return lax.ppermute(value, axis, [(i, i ^ mask) for i in range(count)])]
    ppermute x0 -> x40, starting transfers between devices: none -> 58.3 us  [swap(): return lax.ppermute(value, axis, [(i, i ^ mask) for i in range(count)])]
    reduce_scatter x1 -> x0, waiting for transfers between devices: 40.2 us -> none  [body(): lax.psum_scatter(partial_out, 'tensor', scatter_dimension=2, tiled=True)]
    all_gather x3 -> x0, blocking collectives: 25.9 us -> none  [joined(): pieces = jax.tree.map(lambda part: lax.all_gather(part, axis), value)]
    dot_general x1 -> x4, matrix products: 27.4 us -> 33.2 us  [body(): jnp.einsum('msd,mdv->msv', features, head_parts[k], preferred_element_typ...]
  transfers between devices with their start and end apart: 5 -> 40, of which waited for: 5 -> 10; matrix products, arithmetic and copies ran while one was open for 0% -> 7% of each run, Pallas kernels for 0% -> 0%
where the time goes in v1:
time: 520 us
  waiting for transfers between devices  383 us (74%)
  starting transfers between devices  58.3 us (11%)
  matrix products  42 us (8%)
  other arithmetic  17.6 us (3%)
  local copies, waits for them, and re-layouts  16.5 us (3%)
    ppermute x40, waiting for transfers between devices, swap(): return lax.ppermute(value, axis, [(i, i ^ mask) for i in range(count)])  383 us
    ppermute x40, starting transfers between devices, swap(): return lax.ppermute(value, axis, [(i, i ^ mask) for i in range(count)])  58.3 us
    dot_general x4, matrix products, body(): jnp.einsum('msd,mdv->msv', features, head_parts[k], preferred_element_typ...  33.2 us
  transfers between devices with their start and end apart: 40, of which 10 were waited for; matrix products, arithmetic and copies ran while one was open for 7% of the time, Pallas kernels for 0%

profile of v1, /device:TPU:1, one launch (start us, length us, event | category | flops | bytes accessed | tf_op | source)
XLA Modules:
  0.0 520.0 jit_solution(1303063516044304895)
XLA Ops:
  0.7 1.0 fusion.35
  1.8 0.6 gather_fusion.3
  2.4 4.2 collective-permute-start.2
  7.4 0.6 gather_fusion.1
  8.4 1.2 dynamic_slice.83
  9.6 0.7 compare_and_fusion.7
  10.9 0.7 compare_and_fusion.6
  11.6 5.8 %collective-permute-done.1 = bf16[2,2,64,256]{3,2,0,1:T(8,128)(2,1)S(1)} collective-permute-done((bf16[2,2,64,256]{3,2,0,1:T(8,128)(2,1)S(1)}, bf16[2,2,64,256]{3,2,0,1:T(8,128)(2,1)S(1)}, u32[]{:S(2)}, u32[]{:S(2)}) %collective-permute-start.1) | collective-permute-done | bytes 131104 | tf_op jit(solution)/shard_map/ppermute | solution.py:11
  17.5 0.7 add_convert_fusion.1
  18.2 1.3 collective-permute-start.7
  19.5 1.2 collective-permute-start.5
  20.9 2.2 collective-permute-start.9
  23.1 2.4 collective-permute-start.8
  25.5 3.4 collective-permute-start.6
  29.2 1.5 broadcast_in_dim.104
  30.8 0.6 copy-done.7
  31.5 0.6 copy-done.9
  32.1 1.3 select_dynamic-update-slice_fusion.7
  33.4 1.2 select_dynamic-update-slice_fusion.6
  35.0 8.8 %convolution_add_fusion = f32[2,128,2048]{2,1,0:T(8,128)S(1)} fusion(bf16[2,1024,2048]{2,1,0:T(8,128)(2,1)} %param.20, f32[2,128,2048]{2,1,0:T(8,128)} %broadcast_in_dim.104, pred[2048]{0:T(1024)(128)(4,1)S(1)} %broadcast_in_dim.101, bf16[2,128,2048]{2,1,0:T(8,128)(2,1)S(1)} %select_dynamic-update-slice_fusion, bf16[2,2048,1024]{2,1,0:T(8,128)(2,1)} %param.19), kind=kOutput, calls=%fused_computation.9 | convolution fusion | flops 2149318656 | bytes 22022144 | tf_op jit(solution)/shard_map/msf,mfd->msd/dot_general | solution.py:89
  44.1 1.3 copy-done.2
  46.0 2.3 collective-permute-done.10
  48.3 1.3 bitcast_add_fusion
  49.7 0.6 collective-permute-start.13
  50.3 0.8 collective-permute-start.12
  51.1 1.3 collective-permute-start.11
  52.4 2.1 collective-permute-start.27
  54.5 3.7 collective-permute-done.13
  58.2 5.6 %collective-permute-done.12 = f32[2,16,2048]{2,1,0:T(8,128)S(1)} collective-permute-done((f32[2,16,2048]{2,1,0:T(8,128)S(1)}, f32[2,16,2048]{2,1,0:T(8,128)S(1)}, u32[]{:S(2)}, u32[]{:S(2)}) %collective-permute-start.12) | collective-permute-done | bytes 262176 | tf_op jit(solution)/shard_map/ppermute | solution.py:11
  64.1 2.0 collective-permute-start.14
  66.2 1.6 collective-permute-start.16
  67.7 2.4 collective-permute-done.14
  70.2 7.0 %collective-permute-done.15 = bf16[2,16,2048]{2,1,0:T(8,128)(2,1)S(1)} collective-permute-done((bf16[2,16,2048]{2,1,0:T(8,128)(2,1)S(1)}, bf16[2,16,2048]{2,1,0:T(8,128)(2,1)S(1)}, u32[]{:S(2)}, u32[]{:S(2)}) %collective-permute-start.15) | collective-permute-done | bytes 131104 | tf_op jit(solution)/shard_map/ppermute | solution.py:11
  77.4 0.9 collective-permute-start.21
  78.3 0.7 collective-permute-start.19
  79.0 1.0 collective-permute-start.17
  80.1 0.7 broadcast_compare_fusion
  80.8 1.3 collective-permute-start.23
  82.1 8.4 %collective-permute-done.21 = bf16[2,4,16,2048]{3,2,1,0:T(8,128)(2,1)S(1)} collective-permute-done((bf16[2,4,16,2048]{3,2,1,0:T(8,128)(2,1)S(1)}, bf16[2,4,16,2048]{3,2,1,0:T(8,128)(2,1)S(1)}, u32[]{:S(2)}, u32[]{:S(2)}) %collective-permute-start.21) | collective-permute-done | bytes 524320 | tf_op jit(solution)/shard_map/ppermute | solution.py:11
  90.5 2.1 collective-permute-start.22
  92.6 11.2 %collective-permute-start.20 = (bf16[2,4,16,2048]{3,2,1,0:T(8,128)(2,1)S(1)}, bf16[2,4,16,2048]{3,2,1,0:T(8,128)(2,1)S(1)}, u32[]{:S(2)}, u32[]{:S(2)}) collective-permute-start(bf16[2,4,16,2048]{3,2,1,0:T(8,128)(2,1)S(1)} %collective-permute-done.19), channel_id=1, source_target_pairs={{0,1},{1,0},{2,3},{3,2},{4,5},{5,4},{6,7},{7,6},{8,9},{9,8},{10,11... | collective-permute-start | bytes 1572872 | tf_op jit(solution)/shard_map/ppermute | solution.py:11
  103.9 6.0 %constant_dynamic-slice_fusion.4 = (bf16[2,512,2048]{2,1,0:T(8,128)(2,1)S(1)}, bf16[2,512,2048]{2,1,0:T(8,128)(2,1)S(1)}, bf16[2,512,2048]{2,1,0:T(8,128)(2,1)S(1)}) fusion(bf16[2,512,8192]{2,1,0:T(8,128)(2,1)} %param.23, s32[]{:T(128)S(6)} %select_n.680, s32[]{:T(128)S(6)} %select_n.678, s32[]{:T(128)S(6)} %select_n.676), kind=kLoop, calls=%fused_computation.153 | loop fusion | bytes 25165836 | tf_op jit(solution)/shard_map/dynamic_slice | solution.py:77
  109.9 1.9 collective-permute-start.26
  111.9 1.7 collective-permute-start.24
  113.5 1.0 bitcast_dynamic-update-slice_fusion.6
  114.5 0.9 bitcast_dynamic-update-slice_fusion.5
  117.5 6.1 %fusion = f32[2,512,2048]{2,1,0:T(8,128)S(1)} fusion(bf16[2,512,8192]{2,1,0:T(8,128)(2,1)} %param.23, s32[]{:T(128)S(6)} %select_n.674, bf16[2,512,2048]{2,1,0:T(8,128)(2,1)S(1)} %bitcast.172, s32[]{:T(128)S(6)} %select_n.673), kind=kOutput, calls=%fused_computation.7 | convolution fusion | flops 2147483648 | bytes 13631496 | tf_op jit(solution)/shard_map/msd,mdv->msv/dot_general | solution.py:123
  123.6 346.7 %collective-permute-done.25 = bf16[2,512,2048]{2,1,0:T(8,128)(2,1)S(1)} collective-permute-done((bf16[2,512,2048]{2,1,0:T(8,128)(2,1)S(1)}, bf16[2,512,2048]{2,1,0:T(8,128)(2,1)S(1)}, u32[]{:S(2)}, u32[]{:S(2)}) %collective-permute-start.25) | collective-permute-done | bytes 4194336 | tf_op jit(solution)/shard_map/ppermute | solution.py:11
  470.2 5.6 %fusion.8 = f32[2,512,2048]{2,1,0:T(8,128)} fusion(bf16[2,512,2048]{2,1,0:T(8,128)(2,1)S(1)} %collective-permute-done.25, bf16[2,512,2048]{2,1,0:T(8,128)(2,1)S(1)} %bitcast.173, s32[]{:T(128)S(6)} %select_n.677), kind=kOutput, calls=%fused_computation.17 | convolution fusion | flops 2147483648 | bytes 13631492 | tf_op jit(solution)/shard_map/msd,mdv->msv/dot_general | solution.py:123
  475.9 7.8 %fusion.10 = f32[2,512,2048]{2,1,0:T(8,128)} fusion(bf16[2,512,2048]{2,1,0:T(8,128)(2,1)} %collective-permute-done.24, bf16[2,512,2048]{2,1,0:T(8,128)(2,1)S(1)} %bitcast.174, s32[]{:T(128)S(6)} %select_n.675), kind=kOutput, calls=%fused_computation.19 | convolution fusion | flops 2147483648 | bytes 13631492 | tf_op jit(solution)/shard_map/msd,mdv->msv/dot_general | solution.py:123
  483.7 13.7 %fusion.45 = (f32[2,512]{1,0:T(2,128)S(1)}, f32[2,512,2048]{2,1,0:T(8,128)}) fusion(bf16[2,512,2048]{2,1,0:T(8,128)(2,1)} %collective-permute-done.26, bf16[2,512,2048]{2,1,0:T(8,128)(2,1)} %bitcast.175, s32[]{:T(128)S(6)} %select_n.679, f32[2,512,2048]{2,1,0:T(8,128)} %fusion.8, f32[2,512,2048]{2,1,0:T(8,128)S(1)} %fusion, f32[2,512,2048]{2,1,0:T(8,128)} %fusion.10), kind=kOutput, calls=%fused_computation.230 | convolution fusion | flops 2155871232 | bytes 38801412 | tf_op jit(solution)/shard_map/msd,mdv->msv/dot_general | solution.py:123
  497.4 4.9 select_reduce_fusion
  502.4 1.3 collective-permute-start.30
  503.7 2.3 collective-permute-start.32
  506.0 0.7 collective-permute-done.30
  507.1 1.0 collective-permute-start.37
  508.0 0.8 collective-permute-start.35
  508.8 1.0 collective-permute-start.33
  509.8 3.6 collective-permute-start.39
  513.6 0.8 collective-permute-start.36
  514.4 2.0 collective-permute-start.34
  517.1 0.6 dynamic_slice.84
  518.8 0.6 fusion.38
  519.4 0.6 dynamic-slice_bitcast_fusion.4
  (136 shorter events, 7.4 us)
Async XLA Ops:
  0.6 1.1 copy-start
  2.4 9.1 %collective-permute-start.2 = (bf16[2,2,64,256]{3,2,0,1:T(8,128)(2,1)S(1)}, bf16[2,2,64,256]{3,2,0,1:T(8,128)(2,1)S(1)}, u32[]{:S(2)}, u32[]{:S(2)}) collective-permute-start(bf16[2,2,64,256]{3,2,0,1:T(8,128)(2,1)S(1)} %select_bitcast_fusion), channel_id=1, source_target_pairs={{0,24},{8,16},{16,8},{24,0},{1,25},{9,17},{17,9},{25,1},{2,26},{10... | collective-permute-start | bytes 393224 | tf_op jit(solution)/shard_map/ppermute | solution.py:11
  7.3 10.0 %collective-permute-start.1 = (bf16[2,2,64,256]{3,2,0,1:T(8,128)(2,1)S(1)}, bf16[2,2,64,256]{3,2,0,1:T(8,128)(2,1)S(1)}, u32[]{:S(2)}, u32[]{:S(2)}) collective-permute-start(bf16[2,2,64,256]{3,2,0,1:T(8,128)(2,1)S(1)} %select_bitcast_fusion.1), channel_id=1, source_target_pairs={{0,16},{8,24},{16,0},{24,8},{1,17},{9,25},{17,1},{25,9},{2,18},{10... | collective-permute-start | bytes 393224 | tf_op jit(solution)/shard_map/ppermute | solution.py:11
  8.1 9.3 %collective-permute-start = (bf16[2,2,64,256]{3,2,0,1:T(8,128)(2,1)S(1)}, bf16[2,2,64,256]{3,2,0,1:T(8,128)(2,1)S(1)}, u32[]{:S(2)}, u32[]{:S(2)}) collective-permute-start(bf16[2,2,64,256]{3,2,0,1:T(8,128)(2,1)S(1)} %select_bitcast_fusion.2), channel_id=1, source_target_pairs={{0,8},{8,0},{16,24},{24,16},{1,9},{9,1},{17,25},{25,17},{2,10},{10... | collective-permute-start | bytes 393224 | tf_op jit(solution)/shard_map/ppermute | solution.py:11
  18.2 4.9 collective-permute-start.7
  19.5 6.0 %collective-permute-start.5 = (bf16[2,128,256]{2,1,0:T(8,128)(2,1)S(1)}, bf16[2,128,256]{2,1,0:T(8,128)(2,1)S(1)}, u32[]{:S(2)}, u32[]{:S(2)}) collective-permute-start(bf16[2,128,256]{2,1,0:T(8,128)(2,1)S(1)} %add_convert_fusion.1), channel_id=1, source_target_pairs={{0,4},{1,5},{2,6},{3,7},{4,0},{5,1},{6,2},{7,3},{8,12},{9,13},{10,... | collective-permute-start | bytes 393224 | tf_op jit(solution)/shard_map/ppermute | solution.py:11
  20.7 8.2 %collective-permute-start.3 = (bf16[2,128,256]{2,1,0:T(8,128)(2,1)S(1)}, bf16[2,128,256]{2,1,0:T(8,128)(2,1)S(1)}, u32[]{:S(2)}, u32[]{:S(2)}) collective-permute-start(bf16[2,128,256]{2,1,0:T(8,128)(2,1)S(1)} %add_convert_fusion.1), channel_id=1, source_target_pairs={{0,6},{1,7},{2,4},{3,5},{4,2},{5,3},{6,0},{7,1},{8,14},{9,15},{10,... | collective-permute-start | bytes 393224 | tf_op jit(solution)/shard_map/ppermute | solution.py:11
  20.9 9.9 %collective-permute-start.9 = (bf16[2,128,256]{2,1,0:T(8,128)(2,1)S(1)}, bf16[2,128,256]{2,1,0:T(8,128)(2,1)S(1)}, u32[]{:S(2)}, u32[]{:S(2)}) collective-permute-start(bf16[2,128,256]{2,1,0:T(8,128)(2,1)S(1)} %add_convert_fusion.1), channel_id=1, source_target_pairs={{0,1},{1,0},{2,3},{3,2},{4,5},{5,4},{6,7},{7,6},{8,9},{9,8},{10,11... | collective-permute-start | bytes 393224 | tf_op jit(solution)/shard_map/ppermute | solution.py:11
  23.1 7.7 %copy-start.4 = (bf16[2,128,256]{2,1,0:T(8,128)(2,1)}, bf16[2,128,256]{2,1,0:T(8,128)(2,1)S(1)}, u32[]{:S(2)}) copy-start(bf16[2,128,256]{2,1,0:T(8,128)(2,1)S(1)} %collective-permute-done.7) | copy-start | bytes 393220
  23.1 7.7 %collective-permute-start.8 = (bf16[2,128,256]{2,1,0:T(8,128)(2,1)S(1)}, bf16[2,128,256]{2,1,0:T(8,128)(2,1)S(1)}, u32[]{:S(2)}, u32[]{:S(2)}) collective-permute-start(bf16[2,128,256]{2,1,0:T(8,128)(2,1)S(1)} %collective-permute-done.7), channel_id=1, source_target_pairs={{0,1},{1,0},{2,3},{3,2},{4,5},{5,4},{6,7},{7,6},{8,9},{9,8},{10,11... | collective-permute-start | bytes 393224 | tf_op jit(solution)/shard_map/ppermute | solution.py:11
  25.5 5.3 %copy-start.5 = (bf16[2,128,256]{2,1,0:T(8,128)(2,1)}, bf16[2,128,256]{2,1,0:T(8,128)(2,1)S(1)}, u32[]{:S(2)}) copy-start(bf16[2,128,256]{2,1,0:T(8,128)(2,1)S(1)} %collective-permute-done.5) | copy-start | bytes 393220
  25.5 5.3 %collective-permute-start.6 = (bf16[2,128,256]{2,1,0:T(8,128)(2,1)S(1)}, bf16[2,128,256]{2,1,0:T(8,128)(2,1)S(1)}, u32[]{:S(2)}, u32[]{:S(2)}) collective-permute-start(bf16[2,128,256]{2,1,0:T(8,128)(2,1)S(1)} %collective-permute-done.5), channel_id=1, source_target_pairs={{0,1},{1,0},{2,3},{3,2},{4,5},{5,4},{6,7},{7,6},{8,9},{9,8},{10,11... | collective-permute-start | bytes 393224 | tf_op jit(solution)/shard_map/ppermute | solution.py:11
  28.9 1.9 copy-start.6
  28.9 3.2 collective-permute-start.4
  30.8 0.7 copy-start.7
  30.8 0.7 copy-start.8
  31.5 0.6 copy-start.9
  44.0 8.4 %copy-start.12 = (s32[1,128]{1,0:T(1,128)S(1)}, s32[1,128]{1,0:T(1,128)}, u32[]{:S(2)}) copy-start(s32[1,128]{1,0:T(1,128)} %param.17) | copy-start | bytes 1540
  44.1 1.4 copy-start.2
  44.1 19.9 %copy-start.10 = (f32[2,2048]{1,0:T(2,128)S(1)}, f32[2,2048]{1,0:T(2,128)}, u32[]{:S(2)}) copy-start(f32[2,2048]{1,0:T(2,128)} %param.22) | copy-start | bytes 49156
  44.1 19.9 %copy-start.11 = (f32[2,2048]{1,0:T(2,128)S(1)}, f32[2,2048]{1,0:T(2,128)}, u32[]{:S(2)}) copy-start(f32[2,2048]{1,0:T(2,128)} %param.21) | copy-start | bytes 49156
  45.5 2.8 collective-permute-start.10
  49.7 8.5 %collective-permute-start.13 = (f32[2,16,2048]{2,1,0:T(8,128)S(1)}, f32[2,16,2048]{2,1,0:T(8,128)S(1)}, u32[]{:S(2)}, u32[]{:S(2)}) collective-permute-start(f32[2,16,2048]{2,1,0:T(8,128)S(1)} %get-tuple-element.58), channel_id=1, source_target_pairs={{0,6},{1,7},{2,4},{3,5},{4,2},{5,3},{6,0},{7,1},{8,14},{9,15},{10,... | collective-permute-start | bytes 786440 | tf_op jit(solution)/shard_map/ppermute | solution.py:11
  50.3 13.5 %collective-permute-start.12 = (f32[2,16,2048]{2,1,0:T(8,128)S(1)}, f32[2,16,2048]{2,1,0:T(8,128)S(1)}, u32[]{:S(2)}, u32[]{:S(2)}) collective-permute-start(f32[2,16,2048]{2,1,0:T(8,128)S(1)} %get-tuple-element.59), channel_id=1, source_target_pairs={{0,4},{1,5},{2,6},{3,7},{4,0},{5,1},{6,2},{7,3},{8,12},{9,13},{10,... | collective-permute-start | bytes 786440 | tf_op jit(solution)/shard_map/ppermute | solution.py:11
  51.1 12.7 %collective-permute-start.11 = (f32[2,16,2048]{2,1,0:T(8,128)S(1)}, f32[2,16,2048]{2,1,0:T(8,128)S(1)}, u32[]{:S(2)}, u32[]{:S(2)}) collective-permute-start(f32[2,16,2048]{2,1,0:T(8,128)S(1)} %get-tuple-element.57), channel_id=1, source_target_pairs={{0,2},{1,3},{2,0},{3,1},{4,6},{5,7},{6,4},{7,5},{8,10},{9,11},{10,... | collective-permute-start | bytes 786440 | tf_op jit(solution)/shard_map/ppermute | solution.py:11
  52.4 13.8 %collective-permute-start.27 = (s32[1,128]{1,0:T(1,128)S(1)}, s32[1,128]{1,0:T(1,128)S(1)}, u32[]{:S(2)}, u32[]{:S(2)}) collective-permute-start(s32[1,128]{1,0:T(1,128)S(1)} %copy-done.12), channel_id=1, source_target_pairs={{0,24},{8,16},{16,8},{24,0},{1,25},{9,17},{17,9},{25,1},{2,26},{10... | collective-permute-start | bytes 1544 | tf_op jit(solution)/shard_map/ppermute | solution.py:11
  54.5 13.2 %collective-permute-start.28 = (s32[1,128]{1,0:T(1,128)S(1)}, s32[1,128]{1,0:T(1,128)S(1)}, u32[]{:S(2)}, u32[]{:S(2)}) collective-permute-start(s32[1,128]{1,0:T(1,128)S(1)} %copy-done.12), channel_id=1, source_target_pairs={{0,16},{8,24},{16,0},{24,8},{1,17},{9,25},{17,1},{25,9},{2,18},{10... | collective-permute-start | bytes 1544 | tf_op jit(solution)/shard_map/ppermute | solution.py:11
  58.2 9.5 %collective-permute-start.29 = (s32[1,128]{1,0:T(1,128)S(1)}, s32[1,128]{1,0:T(1,128)S(1)}, u32[]{:S(2)}, u32[]{:S(2)}) collective-permute-start(s32[1,128]{1,0:T(1,128)S(1)} %copy-done.12), channel_id=1, source_target_pairs={{0,8},{8,0},{16,24},{24,16},{1,9},{9,1},{17,25},{25,17},{2,10},{10... | collective-permute-start | bytes 1544 | tf_op jit(solution)/shard_map/ppermute | solution.py:11
  64.1 6.1 %collective-permute-start.14 = (bf16[2,16,2048]{2,1,0:T(8,128)(2,1)S(1)}, bf16[2,16,2048]{2,1,0:T(8,128)(2,1)S(1)}, u32[]{:S(2)}, u32[]{:S(2)}) collective-permute-start(bf16[2,16,2048]{2,1,0:T(8,128)(2,1)S(1)} %add_convert_fusion), channel_id=1, source_target_pairs={{0,24},{8,16},{16,8},{24,0},{1,25},{9,17},{17,9},{25,1},{2,26},{10... | collective-permute-start | bytes 393224 | tf_op jit(solution)/shard_map/ppermute | solution.py:11
  66.2 11.0 %collective-permute-start.15 = (bf16[2,16,2048]{2,1,0:T(8,128)(2,1)S(1)}, bf16[2,16,2048]{2,1,0:T(8,128)(2,1)S(1)}, u32[]{:S(2)}, u32[]{:S(2)}) collective-permute-start(bf16[2,16,2048]{2,1,0:T(8,128)(2,1)S(1)} %add_convert_fusion), channel_id=1, source_target_pairs={{0,16},{8,24},{16,0},{24,8},{1,17},{9,25},{17,1},{25,9},{2,18},{10... | collective-permute-start | bytes 393224 | tf_op jit(solution)/shard_map/ppermute | solution.py:11
  66.2 11.0 %collective-permute-start.16 = (bf16[2,16,2048]{2,1,0:T(8,128)(2,1)S(1)}, bf16[2,16,2048]{2,1,0:T(8,128)(2,1)S(1)}, u32[]{:S(2)}, u32[]{:S(2)}) collective-permute-start(bf16[2,16,2048]{2,1,0:T(8,128)(2,1)S(1)} %add_convert_fusion), channel_id=1, source_target_pairs={{0,8},{8,0},{16,24},{24,16},{1,9},{9,1},{17,25},{25,17},{2,10},{10... | collective-permute-start | bytes 393224 | tf_op jit(solution)/shard_map/ppermute | solution.py:11
  77.4 13.1 %collective-permute-start.21 = (bf16[2,4,16,2048]{3,2,1,0:T(8,128)(2,1)S(1)}, bf16[2,4,16,2048]{3,2,1,0:T(8,128)(2,1)S(1)}, u32[]{:S(2)}, u32[]{:S(2)}) collective-permute-start(bf16[2,4,16,2048]{3,2,1,0:T(8,128)(2,1)S(1)} %pad_maximum_fusion), channel_id=1, source_target_pairs={{0,2},{1,3},{2,0},{3,1},{4,6},{5,7},{6,4},{7,5},{8,10},{9,11},{10,... | collective-permute-start | bytes 1572872 | tf_op jit(solution)/shard_map/ppermute | solution.py:11
  78.3 14.3 %collective-permute-start.19 = (bf16[2,4,16,2048]{3,2,1,0:T(8,128)(2,1)S(1)}, bf16[2,4,16,2048]{3,2,1,0:T(8,128)(2,1)S(1)}, u32[]{:S(2)}, u32[]{:S(2)}) collective-permute-start(bf16[2,4,16,2048]{3,2,1,0:T(8,128)(2,1)S(1)} %pad_maximum_fusion), channel_id=1, source_target_pairs={{0,4},{1,5},{2,6},{3,7},{4,0},{5,1},{6,2},{7,3},{8,12},{9,13},{10,... | collective-permute-start | bytes 1572872 | tf_op jit(solution)/shard_map/ppermute | solution.py:11
  79.0 24.8 %collective-permute-start.17 = (bf16[2,4,16,2048]{3,2,1,0:T(8,128)(2,1)S(1)}, bf16[2,4,16,2048]{3,2,1,0:T(8,128)(2,1)S(1)}, u32[]{:S(2)}, u32[]{:S(2)}) collective-permute-start(bf16[2,4,16,2048]{3,2,1,0:T(8,128)(2,1)S(1)} %pad_maximum_fusion), channel_id=1, source_target_pairs={{0,6},{1,7},{2,4},{3,5},{4,2},{5,3},{6,0},{7,1},{8,14},{9,15},{10,... | collective-permute-start | bytes 1572872 | tf_op jit(solution)/shard_map/ppermute | solution.py:11
  80.8 31.1 %collective-permute-start.23 = (bf16[2,4,16,2048]{3,2,1,0:T(8,128)(2,1)S(1)}, bf16[2,4,16,2048]{3,2,1,0:T(8,128)(2,1)S(1)}, u32[]{:S(2)}, u32[]{:S(2)}) collective-permute-start(bf16[2,4,16,2048]{3,2,1,0:T(8,128)(2,1)S(1)} %pad_maximum_fusion), channel_id=1, source_target_pairs={{0,1},{1,0},{2,3},{3,2},{4,5},{5,4},{6,7},{7,6},{8,9},{9,8},{10,11... | collective-permute-start | bytes 1572872 | tf_op jit(solution)/shard_map/ppermute | solution.py:11
  90.5 21.4 %collective-permute-start.22 = (bf16[2,4,16,2048]{3,2,1,0:T(8,128)(2,1)S(1)}, bf16[2,4,16,2048]{3,2,1,0:T(8,128)(2,1)S(1)}, u32[]{:S(2)}, u32[]{:S(2)}) collective-permute-start(bf16[2,4,16,2048]{3,2,1,0:T(8,128)(2,1)S(1)} %collective-permute-done.21), channel_id=1, source_target_pairs={{0,1},{1,0},{2,3},{3,2},{4,5},{5,4},{6,7},{7,6},{8,9},{9,8},{10,11... | collective-permute-start | bytes 1572872 | tf_op jit(solution)/shard_map/ppermute | solution.py:11
  92.6 20.9 %collective-permute-start.20 = (bf16[2,4,16,2048]{3,2,1,0:T(8,128)(2,1)S(1)}, bf16[2,4,16,2048]{3,2,1,0:T(8,128)(2,1)S(1)}, u32[]{:S(2)}, u32[]{:S(2)}) collective-permute-start(bf16[2,4,16,2048]{3,2,1,0:T(8,128)(2,1)S(1)} %collective-permute-done.19), channel_id=1, source_target_pairs={{0,1},{1,0},{2,3},{3,2},{4,5},{5,4},{6,7},{7,6},{8,9},{9,8},{10,11... | collective-permute-start | bytes 1572872 | tf_op jit(solution)/shard_map/ppermute | solution.py:11
  103.9 9.6 %collective-permute-start.18 = (bf16[2,4,16,2048]{3,2,1,0:T(8,128)(2,1)S(1)}, bf16[2,4,16,2048]{3,2,1,0:T(8,128)(2,1)S(1)}, u32[]{:S(2)}, u32[]{:S(2)}) collective-permute-start(bf16[2,4,16,2048]{3,2,1,0:T(8,128)(2,1)S(1)} %collective-permute-done.17), channel_id=1, source_target_pairs={{0,1},{1,0},{2,3},{3,2},{4,5},{5,4},{6,7},{7,6},{8,9},{9,8},{10,11... | collective-permute-start | bytes 1572872 | tf_op jit(solution)/shard_map/ppermute | solution.py:11
  109.9 373.8 %collective-permute-start.26 = (bf16[2,512,2048]{2,1,0:T(8,128)(2,1)S(1)}, bf16[2,512,2048]{2,1,0:T(8,128)(2,1)}, u32[]{:S(2)}, u32[]{:S(2)}) collective-permute-start(bf16[2,512,2048]{2,1,0:T(8,128)(2,1)S(1)} %get-tuple-element.54), channel_id=1, source_target_pairs={{0,24},{8,16},{16,8},{24,0},{1,25},{9,17},{17,9},{25,1},{2,26},{10... | collective-permute-start | bytes 12582920 | tf_op jit(solution)/shard_map/ppermute | solution.py:11
  111.9 358.4 %collective-permute-start.25 = (bf16[2,512,2048]{2,1,0:T(8,128)(2,1)S(1)}, bf16[2,512,2048]{2,1,0:T(8,128)(2,1)S(1)}, u32[]{:S(2)}, u32[]{:S(2)}) collective-permute-start(bf16[2,512,2048]{2,1,0:T(8,128)(2,1)S(1)} %get-tuple-element.55), channel_id=1, source_target_pairs={{0,16},{8,24},{16,0},{24,8},{1,17},{9,25},{17,1},{25,9},{2,18},{10... | collective-permute-start | bytes 12582920 | tf_op jit(solution)/shard_map/ppermute | solution.py:11
  111.9 364.0 %collective-permute-start.24 = (bf16[2,512,2048]{2,1,0:T(8,128)(2,1)S(1)}, bf16[2,512,2048]{2,1,0:T(8,128)(2,1)}, u32[]{:S(2)}, u32[]{:S(2)}) collective-permute-start(bf16[2,512,2048]{2,1,0:T(8,128)(2,1)S(1)} %get-tuple-element.56), channel_id=1, source_target_pairs={{0,8},{8,0},{16,24},{24,16},{1,9},{9,1},{17,25},{25,17},{2,10},{10... | collective-permute-start | bytes 12582920 | tf_op jit(solution)/shard_map/ppermute | solution.py:11
  117.5 358.4 %copy-start.3 = (bf16[2,4,8,16,2048]{4,3,2,1,0:T(8,128)(2,1)}, bf16[2,4,8,16,2048]{4,3,2,1,0:T(8,128)(2,1)S(1)}, u32[]{:S(2)}) copy-start(bf16[2,4,8,16,2048]{4,3,2,1,0:T(8,128)(2,1)S(1)} %bitcast_dynamic-update-slice_fusion.7) | copy-start | bytes 12582916
  497.4 22.5 %copy-start.1 = (bf16[2,4,64,256]{3,2,1,0:T(8,128)(2,1)S(1)}, bf16[2,4,64,256]{3,2,1,0:T(8,128)(2,1)}, u32[]{:S(2)}) copy-start(bf16[2,4,64,256]{3,2,1,0:T(8,128)(2,1)} %param.13) | copy-start | bytes 786436
  497.4 19.6 %copy-start.13 = (s32[4]{0:T(128)S(1)}, s32[4]{0:T(128)}, u32[]{:S(2)}) copy-start(s32[4]{0:T(128)} %param.16) | copy-start | bytes 52
  502.4 4.3 collective-permute-start.30
  503.7 3.3 collective-permute-start.31
  503.7 3.3 collective-permute-start.32
  507.1 6.3 %collective-permute-start.37 = (f32[4,3,2,128]{3,2,0,1:T(2,128)S(1)}, f32[4,3,2,128]{3,2,0,1:T(2,128)S(1)}, u32[]{:S(2)}, u32[]{:S(2)}) collective-permute-start(f32[4,3,2,128]{3,2,0,1:T(2,128)S(1)} %pad_maximum_fusion.1), channel_id=1, source_target_pairs={{0,2},{1,3},{2,0},{3,1},{4,6},{5,7},{6,4},{7,5},{8,10},{9,11},{10,... | collective-permute-start | bytes 36872 | tf_op jit(solution)/shard_map/ppermute | solution.py:11
  508.0 5.6 %collective-permute-start.35 = (f32[4,3,2,128]{3,2,0,1:T(2,128)S(1)}, f32[4,3,2,128]{3,2,0,1:T(2,128)S(1)}, u32[]{:S(2)}, u32[]{:S(2)}) collective-permute-start(f32[4,3,2,128]{3,2,0,1:T(2,128)S(1)} %pad_maximum_fusion.1), channel_id=1, source_target_pairs={{0,4},{1,5},{2,6},{3,7},{4,0},{5,1},{6,2},{7,3},{8,12},{9,13},{10,... | collective-permute-start | bytes 36872 | tf_op jit(solution)/shard_map/ppermute | solution.py:11
  508.8 5.6 %collective-permute-start.33 = (f32[4,3,2,128]{3,2,0,1:T(2,128)S(1)}, f32[4,3,2,128]{3,2,0,1:T(2,128)S(1)}, u32[]{:S(2)}, u32[]{:S(2)}) collective-permute-start(f32[4,3,2,128]{3,2,0,1:T(2,128)S(1)} %pad_maximum_fusion.1), channel_id=1, source_target_pairs={{0,6},{1,7},{2,4},{3,5},{4,2},{5,3},{6,0},{7,1},{8,14},{9,15},{10,... | collective-permute-start | bytes 36872 | tf_op jit(solution)/shard_map/ppermute | solution.py:11
  509.8 8.6 %collective-permute-start.39 = (f32[4,3,2,128]{3,2,0,1:T(2,128)S(1)}, f32[4,3,2,128]{3,2,0,1:T(2,128)S(1)}, u32[]{:S(2)}, u32[]{:S(2)}) collective-permute-start(f32[4,3,2,128]{3,2,0,1:T(2,128)S(1)} %pad_maximum_fusion.1), channel_id=1, source_target_pairs={{0,1},{1,0},{2,3},{3,2},{4,5},{5,4},{6,7},{7,6},{8,9},{9,8},{10,11... | collective-permute-start | bytes 36872 | tf_op jit(solution)/shard_map/ppermute | solution.py:11
  513.4 4.9 collective-permute-start.38
  513.6 4.7 collective-permute-start.36
  514.4 4.0 collective-permute-start.34

commit v2 on v1

v2 whole, which is shorter than its diff:
```python
import functools

import jax
import jax.numpy as jnp
from jax import lax
from jax.experimental.layout import Layout, with_layout_constraint
from jax.sharding import PartitionSpec as P

epsilon = 1e-05


def swap(value, axis, mask):
    count = lax.axis_size(axis)
    return lax.ppermute(value, axis, [(i, i ^ mask) for i in range(count)])


def ordered(pieces, index):
    pieces = list(pieces)
    bit = 1
    while bit < len(pieces):
        flip = (index & bit) != 0
        pieces = [jnp.where(flip, pieces[k ^ bit], pieces[k]) for k in range(len(pieces))]
        bit *= 2
    return pieces


def gather_chips(value):
    count = lax.axis_size("tensor")
    far = [value] + [swap(value, "tensor", k) for k in range(2, count, 2)]
    pieces = []
    for piece in far:
        pieces += [piece, swap(piece, "tensor", 1)]
    return pieces


def plain(value):
    return with_layout_constraint(value, Layout(major_to_minor=tuple(range(value.ndim))))


def spread(value, axis):
    return [value] + [swap(value, axis, k) for k in range(1, lax.axis_size(axis))]


def routes(models):
    bits = lax.axis_size("tensor").bit_length() - 1
    return [[1 + (b + m) % (bits - 1) for b in range(bits - 1)] for m in range(models)]


def gather_tensor(value, place, route):
    bits = route + [0]
    for bit in bits:
        other = swap(value, "tensor", 1 << bit)
        flip = ((place >> bit) & 1) != 0
        value = jnp.stack([jnp.where(flip, other, value), jnp.where(flip, value, other)])
    seen = bits[::-1]
    order = [seen.index(b) for b in sorted(bits, reverse=True)]
    rest = list(range(len(bits), value.ndim))
    value = value.transpose(order + rest)
    return value.reshape((1 << len(bits),) + value.shape[len(bits) :])


def scatter_tensor(value, place, route):
    count = value.shape[0]
    left = list(range(count.bit_length() - 2, -1, -1))
    value = value.reshape((2,) * len(left) + value.shape[1:])
    for bit in [0] + route:
        axis = left.index(bit)
        mine = (place >> bit) & 1
        keep = lax.dynamic_index_in_dim(value, mine, axis, False)
        give = lax.dynamic_index_in_dim(value, 1 - mine, axis, False)
        value = keep + swap(give, "tensor", 1 << bit)
        left.remove(bit)
    return value


def section(live, work, *operands):
    shapes = jax.eval_shape(work, *operands)
    idle = lambda *_: jax.tree.map(lambda s: jnp.zeros(s.shape, s.dtype), shapes)
    return lax.cond(live, work, idle, *operands)


def reduced(logits, first, wanted):
    matches = (jnp.arange(logits.shape[-1]) + first)[None, :] == wanted[:, None]
    peak = jnp.max(logits, axis=-1)
    totals = jnp.sum(jnp.exp(logits - peak[..., None]), axis=-1)
    return peak, totals, jnp.sum(jnp.where(matches, logits, 0.0), axis=-1)


def both(one, other):
    peak = jnp.maximum(one[0], other[0])
    totals = one[1] * jnp.exp(one[0] - peak) + other[1] * jnp.exp(other[0] - peak)
    return peak, totals, one[2] + other[2]


lowest = -3e38
steps = 8


def chained(rows, everything, head, targets, lengths, vocab_first, near, far, early, late, part, beside):
    layer = lax.axis_index("dp")
    models, depth = head.shape[:2]
    slot_count = everything.shape[1] // lengths.shape[0]
    outer = jnp.logical_or(layer == 0, layer == 3)
    ends = jnp.cumsum(lengths)
    starts = ends - lengths
    packed = jnp.arange(rows)
    rollout = jnp.sum(packed[:, None] >= ends[None, :], axis=1)
    offset = jnp.sum(
        jnp.where(rollout[:, None] == jnp.arange(lengths.shape[0])[None, :], starts[None, :], 0), axis=1
    )
    source = jnp.where(packed < ends[-1], rollout * slot_count + packed - offset, -1)
    picks = source[:, None] == jnp.arange(everything.shape[1])[None, :]
    wanted = jnp.sum(jnp.where(picks, targets[None, :], 0), axis=1)
    features = lax.dynamic_slice_in_dim(everything, layer * depth, depth, 2)
    features = jnp.einsum(
        "kt,mtd->mkd", picks.astype(jnp.bfloat16), features, preferred_element_type=jnp.float32
    ).astype(jnp.bfloat16)
    features = [features[m] for m in range(models)]
    width = part // steps

    def product(model, first):
        columns = lax.dynamic_slice(head, (model, 0, first), (1, depth, width))[0]
        return jnp.dot(features[model], columns, preferred_element_type=jnp.float32)

    into, out = [(0, 1), (3, 2)], [(1, 0), (2, 3)]
    side = [None] * models
    middle = [None] * models
    found = [[] for _ in range(models)]
    for s in range(-1, steps + 1):
        for m in range(models):
            if s >= 0:
                features[m], side[m], middle[m] = lax.optimization_barrier(
                    (features[m], side[m], middle[m])
                )
            first = jnp.where(outer, far + (s + 1) * width, near + (s - 1) * width)
            give = product(m, first)
            if s >= 1:
                give = give + jnp.where(outer, 0.0, middle[m])
            perm = (into if s + 1 < steps else []) + (out if s >= 1 else [])
            got = lax.ppermute(give, "dp", perm)
            if 0 <= s < steps:
                middle[m] = lax.ppermute(
                    side[m] + product(m, far + s * width), "dp", [(1, 2), (2, 1)]
                )
            side[m] = got
            if s >= 1:
                begin = near + (s - 1) * width
                found[m].append(reduced(got + product(m, begin), vocab_first + begin, wanted))
        if s == 1:
            everything, side = lax.optimization_barrier((everything, side))
            aside = jnp.stack(beside(everything, early, late))
    each = []
    for m in range(models):
        total = found[m][0]
        for more in found[m][1:]:
            total = both(total, more)
        each.append(total)
    peak, totals, target_logit = [jnp.stack(t) for t in zip(*each)]
    stats = jnp.stack(
        [
            jnp.where(outer, peak, lowest),
            jnp.where(outer, totals, 0.0),
            jnp.where(outer, target_logit, 0.0),
        ]
    )
    stats = jnp.pad(stats, ((0, 0), (0, 0), (0, slot_count)))
    stats = jnp.stack(
        [lax.dynamic_slice_in_dim(stats, starts[r], slot_count, 2) for r in range(lengths.shape[0])],
        axis=2,
    )
    return jnp.stack(both(stats, aside.reshape(stats.shape)))


def body(
    pages,
    page_table,
    page_count,
    last_len,
    targets,
    mix_key,
    w_key,
    w_value,
    ln_gain,
    ln_bias,
    head,
):
    tensor_count = lax.axis_size("tensor")
    layer_count = lax.axis_size("dp")
    layer = lax.axis_index("dp")
    place = lax.axis_index("tensor")
    models, rows_held, page_len, width_local = pages.shape
    width = ln_gain.shape[1]
    page_cap = page_table.shape[1]
    slot_count = page_cap * page_len
    share = slot_count // tensor_count
    depth = head.shape[1]
    vocab_held = head.shape[2]
    vocab_part = vocab_held // layer_count

    states = None
    own_rows = page_table[layer]
    for k in range(layer_count):
        wanted = page_table[layer ^ k]
        block = jnp.take(pages, wanted % rows_held, axis=1)
        got = block if k == 0 else swap(block, "dp", k)
        here = (own_rows // rows_held) == (layer ^ k)
        here = jnp.logical_and(here, jnp.arange(page_cap) < page_count[layer])
        got = jnp.where(here[None, :, None, None], got, jnp.zeros_like(got))
        states = got if states is None else states + got

    lengths = (page_count - 1) * page_len + last_len
    wanted = jnp.concatenate(ordered(spread(targets, "dp"), layer), axis=0).reshape(-1)
    head, states, wanted = lax.optimization_barrier((head, states, wanted))

    chain = layer_count == 4
    whole = vocab_part // 4 if chain else vocab_part

    def columns(first, count):
        parts = []
        for k in range(layer_count):
            start = (layer ^ k) * whole + first
            part = plain(lax.dynamic_slice_in_dim(head, start, count, 2))
            parts.append(part if k == 0 else plain(swap(part, "dp", k)))
        return parts

    split = whole // 2
    early = columns(0, split)
    live = page_count[0] > 0
    tracks = routes(models)

    states = states.reshape(models, slot_count, width_local)
    state_f = states.astype(jnp.float32)
    previous = jnp.concatenate(
        [jnp.zeros((models, 1, width_local), jnp.float32), state_f[:, :-1]], axis=1
    )
    shifted = (state_f + (previous - state_f) * mix_key[:, None, :]).astype(jnp.bfloat16)

    def mix(shifted, state_f):
        mine = (jnp.arange(tensor_count) == place)[None, None, :, None]
        value = jnp.stack([gather_tensor(shifted[m], place, tracks[m]) for m in range(models)])
        value = value.transpose(0, 2, 1, 3).reshape(models, slot_count, width)
        hidden = jnp.einsum("msd,mdf->msf", value, w_key, preferred_element_type=jnp.float32)
        key_act = (jnp.maximum(hidden, 0.0) ** 2).astype(jnp.bfloat16)
        mixed = jnp.einsum("msf,mfd->msd", key_act, w_value, preferred_element_type=jnp.float32)
        mixed = mixed.reshape(models, slot_count, tensor_count, width_local)
        mixed = mixed + jnp.where(mine, state_f[:, :, None, :], 0.0)
        mixed = mixed.reshape(models, tensor_count, share, width)
        rows = []
        for m in range(models):
            residual = scatter_tensor(mixed[m], place, tracks[m])
            average = jnp.sum(residual, axis=-1) / width
            variance = jnp.sum(residual * residual, axis=-1) / width - average * average
            normed = (
                (residual - average[..., None]) * lax.rsqrt(variance + epsilon)[..., None]
            ) * ln_gain[m] + ln_bias[m]
            rows.append(normed.astype(jnp.bfloat16))
        return jnp.stack(rows)

    normed = section(live, mix, shifted, state_f)
    normed, early = lax.optimization_barrier((normed, early))
    layers = jnp.stack(ordered(spread(normed, "dp"), layer), axis=1)
    layers, head = lax.optimization_barrier((layers, head))
    late = columns(split, whole - split)

    def everywhere(column):
        values = []
        for m in range(models):
            value = gather_tensor(column[m], place, tracks[m]).transpose(1, 0, 2, 3)
            values.append(value.reshape(layer_count * slot_count, width))
        return jnp.stack(values)

    everything = section(live, everywhere, layers)

    def statistics(features, parts, first):
        logits = None
        for k in range(layer_count):
            rows = lax.dynamic_slice_in_dim(features, (layer ^ k) * depth, depth, 2)
            term = jnp.einsum("msd,mdv->msv", rows, parts[k], preferred_element_type=jnp.float32)
            logits = term if logits is None else logits + term
        start = place * vocab_held + layer * whole + first
        return reduced(logits, start, wanted)

    everything, early, late = lax.optimization_barrier((everything, early, late))
    if chain:
        part = (vocab_held - layer_count * whole) // 2
        low = layer < 2
        near = layer_count * whole + jnp.where(low, 0, part)
        far = layer_count * whole + jnp.where(low, part, 0)
        sizes = [224, 256, 288, 320, 352, 384, layer_count * slot_count]
        beside = lambda value, e, l: both(statistics(value, e, 0), statistics(value, l, split))
        branches = [
            functools.partial(chained, rows, part=part, beside=beside) for rows in sizes
        ]
        bucket = sum((jnp.sum(lengths) > size).astype(jnp.int32) for size in sizes[:-1])
        stats = lax.switch(
            bucket,
            branches,
            everything,
            head,
            wanted,
            lengths,
            place * vocab_held,
            near,
            far,
            early,
            late,
        )
    else:
        stats = both(statistics(everything, early, 0), statistics(everything, late, split))
        stats = jnp.stack(stats).reshape(3, models, layer_count, slot_count)

    stats = stats.reshape(3, models, layer_count, slot_count)
    mine = []
    for k in range(layer_count):
        part = lax.dynamic_index_in_dim(stats, layer ^ k, 2, False)
        mine.append(part if k == 0 else swap(part, "dp", k))
    mine = jnp.concatenate(ordered(gather_chips(jnp.stack(ordered(mine, layer))), place))
    top = jnp.max(mine[:, 0], axis=0)
    totals = jnp.sum(mine[:, 1] * jnp.exp(mine[:, 0] - top), axis=0)
    logp = jnp.sum(mine[:, 2], axis=0) - top - jnp.log(totals)

    valid = jnp.arange(slot_count) < lengths[layer]
    policy_row = jnp.where(valid, logp[0], 0.0)
    ratio = jnp.sum(jnp.where(valid, logp[0] - logp[1], 0.0))
    token_part = lax.dynamic_slice_in_dim(policy_row, place * share, share)[None, :]
    return (token_part, ratio[None])


def solution(mesh):
    placed = (
        P(None, "dp", None, "tensor"),
        P(),
        P(),
        P(),
        P("dp", None),
        P(None, "tensor"),
        P(None, None, "tensor"),
        P(None, "tensor", None),
        P(),
        P(),
        P(None, "dp", "tensor"),
    )
    return jax.shard_map(
        body, mesh=mesh, in_specs=placed, out_specs=(P("dp", "tensor"), P("dp")), check_vma=False
    )
```

time: 520 us -> 459 us (0.88)
  waiting for transfers between devices: 383 us -> 113 us
  starting transfers between devices: 58.3 us -> 128 us
  matrix products: 42 us -> 101 us
  loops' own time: 0 us -> 47 us
  other arithmetic: 17.6 us -> 38.3 us
  local copies, waits for them, and re-layouts: 16.5 us -> 31 us
    ppermute x40 -> x43, waiting for transfers between devices: 383 us -> 48.6 us  [swap(): return lax.ppermute(value, axis, [(i, i ^ mask) for i in range(count)])]
    ppermute x0 -> x36, starting transfers between devices: none -> 65.5 us  [the longest x20 50.9 us: chained(): got = lax.ppermute(give, 'dp', perm)]
    ppermute x0 -> x36, waiting for transfers between devices: none -> 64.8 us  [the longest x20 64.7 us: chained(): got = lax.ppermute(give, 'dp', perm)]
    dot_general x5 -> x62, matrix products: 42 us -> 101 us  [the longest x52 80.4 us: product(): return jnp.dot(features[model], columns, preferred_element_type=jnp.float32)]
    another operation x0 -> x3, loops' own time: none -> 47 us  [the longest x1 46.4 us: body(): lax.switch(bucket, branches, everything, head, wanted, lengths, place * v...]
    another operation x3 -> x30, other arithmetic: 0.55 us -> 12.4 us  [the longest x18 8.66 us: gather_tensor(): jnp.stack([jnp.where(flip, other, value), jnp.where(flip, value, other)])]
    add x2 -> x34, other arithmetic: 1.34 us -> 13.2 us  [the longest x16 10.4 us: chained(): side[m] + product(m, far + s * width)]
    squeeze x2 -> x11, local copies, waits for them, and re-layouts: 0.13 us -> 10 us  [the longest x2 4.74 us: scatter_tensor(): value = value.reshape((2,) * len(left) + value.shape[1:])]
  transfers between devices with their start and end apart: 40 -> 79, of which waited for: 10 -> 32; matrix products, arithmetic and copies ran while one was open for 7% -> 32% of each run, Pallas kernels for 0% -> 0%
where the time goes in v2:
time: 459 us; the launch traced here: 464 us
  starting transfers between devices  128 us (28%)
  waiting for transfers between devices  113 us (25%)
  matrix products  101 us (22%)
  loops' own time  47 us (10%)
  other arithmetic  38.3 us (8%)
  local copies, waits for them, and re-layouts  31 us (7%)
  between operations  5.64 us (1%)
    dot_general x52, matrix products, product(): return jnp.dot(features[model], columns, preferred_element_type=jnp.float32)  80.4 us
    ppermute x20, waiting for transfers between devices, chained(): got = lax.ppermute(give, 'dp', perm)  64.7 us
    ppermute x43, starting transfers between devices, swap(): return lax.ppermute(value, axis, [(i, i ^ mask) for i in range(count)])  62.3 us
    ppermute x20, starting transfers between devices, chained(): got = lax.ppermute(give, 'dp', perm)  50.9 us
    ppermute x43, waiting for transfers between devices, swap(): return lax.ppermute(value, axis, [(i, i ^ mask) for i in range(count)])  48.6 us
    another operation x1, loops' own time, body(): lax.switch(bucket, branches, everything, head, wanted, lengths, place * v...  46.4 us
    ppermute x16, starting transfers between devices, chained(): lax.ppermute(side[m] + product(m, far + s * width), 'dp', [(1, 2), (2, 1)])  14.6 us
    add x16, other arithmetic, chained(): side[m] + product(m, far + s * width)  10.4 us
  transfers between devices with their start and end apart: 79, of which 32 were waited for; matrix products, arithmetic and copies ran while one was open for 32% of the time, Pallas kernels for 0%

profile of v2, /device:TPU:1, one launch (start us, length us, event | category | flops | bytes accessed | tf_op | source)
XLA Modules:
  0.0 463.7 jit_solution(14995219591335149008)
XLA Ops:
  0.6 4.2 collective-permute-start.273
  7.0 2.1 collective-permute-start.271
  16.0 2.1 collective-permute-done.271
  18.1 2.8 collective-permute-done.270
  21.0 2.8 constant_dynamic-slice_fusion.36
  24.6 3.2 collective-permute-start.277
  29.3 57.9 %conditional.3 = (bf16[2,16,2048]{2,1,0:T(8,128)(2,1)S(1)}) conditional(s32[]{:T(128)} %bitcast.662, () %tuple.180, (s32[]{:T(128)}, bf16[2,128,256]{2,1,0:T(8,128)(2,1)S(1)}, bf16[2,2048,1024]{2,1,0:T(8,128)(2,1)}, bf16[2,1024,2048]{2,1,0:T(8,128)(2,1)}, f32[2,128,256]{2,1,0:T(8,128)S(1)}, /*index=5*/f32[2,2048]{1,0:T(2,128)}, ...), branch_computations={%region_1.3_spmd, %region_2.8_spmd} | conditional | flops 2153119744 | bytes 70879160 | solution.py:79
  35.7 2.5 collective-permute-done.259
  39.6 4.1 collective-permute-start.263
  47.3 2.3 copy.365
  49.6 9.9 %fusion.2 = f32[2,128,2048]{2,1,0:T(8,128)} fusion(bf16[2,1024,2048]{2,1,0:T(8,128)(2,1)} %get-tuple-element.815, bf16[2,128,2048]{1,2,0:T(8,128)(2,1)} %bitcast.2274, bf16[2,2048,1024]{2,1,0:T(8,128)(2,1)} %get-tuple-element.814), kind=kOutput, calls=%fused_computation.9 | convolution fusion | flops 2148270080 | bytes 19922944 | tf_op jit(solution)/shard_map/cond/branch_1_fun/msf,mfd->msd/dot_general | solution.py:244
  59.5 2.5 copy.573
  63.9 2.4 squeeze.760
  66.2 1.9 dynamic-slice_bitcast_fusion.1
  68.5 2.4 squeeze.868
  75.4 5.5 %collective-permute-done.265 = f32[2,16,2048]{2,1,0:T(8,128)S(1)} collective-permute-done((f32[2,16,2048]{2,1,0:T(8,128)S(1)}, f32[2,16,2048]{2,1,0:T(8,128)S(1)}, u32[]{:S(2)}, u32[]{:S(2)}) %collective-permute-start.265) | collective-permute-done | bytes 262176 | tf_op jit(solution)/shard_map/cond/branch_1_fun/ppermute | solution.py:14
  85.0 1.8 collective-permute-done.269
  87.2 3.0 collective-permute-start.279
  90.8 2.2 collective-permute-done.279
  93.0 7.3 %collective-permute-done.280 = bf16[2,16,2048]{2,1,0:T(8,128)(2,1)S(1)} collective-permute-done((bf16[2,16,2048]{2,1,0:T(8,128)(2,1)S(1)}, bf16[2,16,2048]{2,1,0:T(8,128)(2,1)S(1)}, u32[]{:S(2)}, u32[]{:S(2)}) %collective-permute-start.280) | collective-permute-done | bytes 131104 | tf_op jit(solution)/shard_map/ppermute | solution.py:14
  101.3 2.7 constant_dynamic-slice_fusion.32
  104.0 1.8 collective-permute-start.283
  105.8 1.8 collective-permute-start.284
  111.9 34.6 %conditional.4 = (bf16[2,512,2048]{2,1,0:T(8,128)(2,1)}) conditional(s32[]{:T(128)} %bitcast.662, () %tuple.179, (s32[]{:T(128)}, bf16[2,4,16,2048]{3,2,1,0:T(8,128)(2,1)}) %tuple.185), branch_computations={%region_7.9_spmd, %region_8.10_spmd} | conditional | flops 11010057 | bytes 75497960 | solution.py:79
  114.0 5.0 %collective-permute-done = bf16[4,16,2048]{2,1,0:T(8,128)(2,1)S(1)} collective-permute-done((bf16[4,16,2048]{2,1,0:T(8,128)(2,1)S(1)}, bf16[4,16,2048]{2,1,0:T(8,128)(2,1)S(1)}, u32[]{:S(2)}, u32[]{:S(2)}) %collective-permute-start) | collective-permute-done | bytes 262176 | tf_op jit(solution)/shard_map/cond/branch_1_fun/ppermute | solution.py:14
  122.2 9.0 %collective-permute-done.1 = bf16[2,4,16,2048]{3,2,1,0:T(8,128)(2,1)S(1)} collective-permute-done((bf16[2,4,16,2048]{3,2,1,0:T(8,128)(2,1)S(1)}, bf16[2,4,16,2048]{3,2,1,0:T(8,128)(2,1)S(1)}, u32[]{:S(2)}, u32[]{:S(2)}) %collective-permute-start.1) | collective-permute-done | bytes 524320 | tf_op jit(solution)/shard_map/cond/branch_1_fun/ppermute | solution.py:14
  132.7 4.5 collective-permute-start.2
  144.1 2.3 pad_maximum_fusion.6
  146.5 286.3 %conditional.5 = (f32[3,2,4,128]{3,2,1,0:T(4,128)S(1)}) conditional(s32[]{:T(128)} %clamp.3, (bf16[2,512,2048]{2,1,0:T(8,128)(2,1)}, s32[4]{0:T(128)S(1)}, s32[]{:T(128)}, s32[]{:T(128)}, bf16[2,512,8192]{2,1,0:T(8,128)(2,1)}, /*index=5*/s32[]{:T(128)}, s32[512]{0:T(512)S(1)}, s32[]{:T(128)}, ...), branch_computations={%region_9.69_spmd, %region_68.128_spmd, %region_127.187_spmd, %reg... | conditional | flops 13189351424 | bytes 387504128 | solution.py:295
  176.7 1.8 fusion.979
  178.5 2.6 fusion.1071
  181.1 6.8 %collective-permute-start.154 = (f32[352,384]{1,0:T(8,128)}, f32[352,384]{1,0:T(8,128)}, u32[]{:S(2)}, u32[]{:S(2)}) collective-permute-start(f32[352,384]{1,0:T(8,128)} %fusion.1071), channel_id=1, source_target_pairs={{0,8},{24,16},{1,9},{25,17},{2,10},{26,18},{3,11},{27,19},{4,12},{... | collective-permute-start | bytes 1622024 | tf_op jit(solution)/shard_map/cond/branch_4_fun/ppermute | solution.py:140
  187.9 2.3 fusion.1079
  190.2 2.1 collective-permute-start.150
  194.2 1.9 collective-permute-done.154
  197.5 1.9 add.7260
  200.8 2.3 fusion.1069
  203.1 5.4 %collective-permute-start.155 = (f32[352,384]{1,0:T(8,128)}, f32[352,384]{1,0:T(8,128)}, u32[]{:S(2)}, u32[]{:S(2)}) collective-permute-start(f32[352,384]{1,0:T(8,128)} %fusion.1069), channel_id=1, source_target_pairs={{0,8},{24,16},{1,9},{25,17},{2,10},{26,18},{3,11},{27,19},{4,12},{... | collective-permute-start | bytes 1622024 | tf_op jit(solution)/shard_map/cond/branch_4_fun/ppermute | solution.py:140
  209.8 1.9 add.7254
  213.2 2.3 fusion.1077
  215.5 4.6 collective-permute-start.151
  231.7 2.4 collective-permute-start.153
  241.7 11.6 %collective-permute-done.153 = f32[352,384]{1,0:T(8,128)S(1)} collective-permute-done((f32[352,384]{1,0:T(8,128)S(1)}, f32[352,384]{1,0:T(8,128)S(1)}, u32[]{:S(2)}, u32[]{:S(2)}) %collective-permute-start.153) | collective-permute-done | bytes 540704 | tf_op jit(solution)/shard_map/cond/branch_4_fun/ppermute | solution.py:140
  257.0 2.3 convolution_add_fusion.171
  259.3 3.8 collective-permute-start.173
  263.0 1.8 fusion.987
  270.1 2.3 convolution_add_fusion.186
  279.3 2.2 fusion.1807
  287.6 2.6 collective-permute-start.175
  294.9 2.5 collective-permute-start.161
  302.2 8.0 %collective-permute-done.161 = f32[352,384]{1,0:T(8,128)S(1)} collective-permute-done((f32[352,384]{1,0:T(8,128)S(1)}, f32[352,384]{1,0:T(8,128)S(1)}, u32[]{:S(2)}, u32[]{:S(2)}) %collective-permute-start.161) | collective-permute-done | bytes 540704 | tf_op jit(solution)/shard_map/cond/branch_4_fun/ppermute | solution.py:140
  315.2 3.1 collective-permute-start.163
  325.6 4.0 collective-permute-start.179
  329.6 3.7 collective-permute-done.163
  337.0 3.2 collective-permute-start.165
  344.5 6.7 %collective-permute-done.165 = f32[352,384]{1,0:T(8,128)S(1)} collective-permute-done((f32[352,384]{1,0:T(8,128)S(1)}, f32[352,384]{1,0:T(8,128)S(1)}, u32[]{:S(2)}, u32[]{:S(2)}) %collective-permute-start.165) | collective-permute-done | bytes 540704 | tf_op jit(solution)/shard_map/cond/branch_4_fun/ppermute | solution.py:140
  352.7 2.6 collective-permute-start.167
  370.5 3.1 collective-permute-done.181
  382.8 6.7 %collective-permute-done.169 = f32[352,384]{1,0:T(8,128)S(1)} collective-permute-done((f32[352,384]{1,0:T(8,128)S(1)}, f32[352,384]{1,0:T(8,128)S(1)}, u32[]{:S(2)}, u32[]{:S(2)}) %collective-permute-start.169) | collective-permute-done | bytes 540704 | tf_op jit(solution)/shard_map/cond/branch_4_fun/ppermute | solution.py:140
  392.3 6.4 %collective-permute-done.183 = f32[352,384]{1,0:T(8,128)S(1)} collective-permute-done((f32[352,384]{1,0:T(8,128)S(1)}, f32[352,384]{1,0:T(8,128)S(1)}, u32[]{:S(2)}, u32[]{:S(2)}) %collective-permute-start.183) | collective-permute-done | bytes 540704 | tf_op jit(solution)/shard_map/cond/branch_4_fun/ppermute | solution.py:140
  404.4 4.3 collective-permute-done.171
  410.1 10.1 %collective-permute-done.185 = f32[352,384]{1,0:T(8,128)S(1)} collective-permute-done((f32[352,384]{1,0:T(8,128)S(1)}, f32[352,384]{1,0:T(8,128)S(1)}, u32[]{:S(2)}, u32[]{:S(2)}) %collective-permute-start.185) | collective-permute-done | bytes 540704 | tf_op jit(solution)/shard_map/cond/branch_4_fun/ppermute | solution.py:140
  434.0 2.4 collective-permute-start.287
  440.1 17.6 %collective-permute-start.294 = (f32[4,3,2,128]{3,2,0,1:T(2,128)S(1)}, f32[4,3,2,128]{3,2,0,1:T(2,128)S(1)}, u32[]{:S(2)}, u32[]{:S(2)}) collective-permute-start(f32[4,3,2,128]{3,2,0,1:T(2,128)S(1)} %pad_maximum_fusion.27), channel_id=1, source_target_pairs={{0,1},{1,0},{2,3},{3,2},{4,5},{5,4},{6,7},{7,6},{8,9},{9,8},{10,11... | collective-permute-start | bytes 36872 | tf_op jit(solution)/shard_map/ppermute | solution.py:14
  (350 shorter events, 169.8 us)
Async XLA Ops:
  0.6 14.3 %collective-permute-start.273 = (s32[1,128]{1,0:T(1,128)}, s32[1,128]{1,0:T(1,128)S(1)}, u32[]{:S(2)}, u32[]{:S(2)}) collective-permute-start(s32[1,128]{1,0:T(1,128)} %param.28), channel_id=1, source_target_pairs={{0,24},{8,16},{16,8},{24,0},{1,25},{9,17},{17,9},{25,1},{2,26},{10... | collective-permute-start | bytes 1544 | tf_op jit(solution)/shard_map/ppermute | solution.py:14
  4.9 10.4 %collective-permute-start.274 = (s32[1,128]{1,0:T(1,128)}, s32[1,128]{1,0:T(1,128)S(1)}, u32[]{:S(2)}, u32[]{:S(2)}) collective-permute-start(s32[1,128]{1,0:T(1,128)} %param.28), channel_id=1, source_target_pairs={{0,16},{8,24},{16,0},{24,8},{1,17},{9,25},{17,1},{25,9},{2,18},{10... | collective-permute-start | bytes 1544 | tf_op jit(solution)/shard_map/ppermute | solution.py:14
  4.9 10.4 %collective-permute-start.275 = (s32[1,128]{1,0:T(1,128)}, s32[1,128]{1,0:T(1,128)S(1)}, u32[]{:S(2)}, u32[]{:S(2)}) collective-permute-start(s32[1,128]{1,0:T(1,128)} %param.28), channel_id=1, source_target_pairs={{0,8},{8,0},{16,24},{24,16},{1,9},{9,1},{17,25},{25,17},{2,10},{10... | collective-permute-start | bytes 1544 | tf_op jit(solution)/shard_map/ppermute | solution.py:14
  7.0 11.1 %collective-permute-start.271 = (bf16[2,2,64,256]{3,2,0,1:T(8,128)(2,1)S(1)}, bf16[2,2,64,256]{3,2,0,1:T(8,128)(2,1)S(1)}, u32[]{:S(2)}, u32[]{:S(2)}) collective-permute-start(bf16[2,2,64,256]{3,2,0,1:T(8,128)(2,1)S(1)} %select_bitcast_fusion.25), channel_id=1, source_target_pairs={{0,16},{8,24},{16,0},{24,8},{1,17},{9,25},{17,1},{25,9},{2,18},{10... | collective-permute-start | bytes 393224 | tf_op jit(solution)/shard_map/ppermute | solution.py:14
  9.7 8.4 %collective-permute-start.272 = (bf16[2,2,64,256]{3,2,0,1:T(8,128)(2,1)S(1)}, bf16[2,2,64,256]{3,2,0,1:T(8,128)(2,1)S(1)}, u32[]{:S(2)}, u32[]{:S(2)}) collective-permute-start(bf16[2,2,64,256]{3,2,0,1:T(8,128)(2,1)S(1)} %select_bitcast_fusion.24), channel_id=1, source_target_pairs={{0,24},{8,16},{16,8},{24,0},{1,25},{9,17},{17,9},{25,1},{2,26},{10... | collective-permute-start | bytes 393224 | tf_op jit(solution)/shard_map/ppermute | solution.py:14
  14.9 6.0 %collective-permute-start.270 = (bf16[2,2,64,256]{3,2,0,1:T(8,128)(2,1)S(1)}, bf16[2,2,64,256]{3,2,0,1:T(8,128)(2,1)S(1)}, u32[]{:S(2)}, u32[]{:S(2)}) collective-permute-start(bf16[2,2,64,256]{3,2,0,1:T(8,128)(2,1)S(1)} %select_bitcast_fusion.26), channel_id=1, source_target_pairs={{0,8},{8,0},{16,24},{24,16},{1,9},{9,1},{17,25},{25,17},{2,10},{10... | collective-permute-start | bytes 393224 | tf_op jit(solution)/shard_map/ppermute | solution.py:14
  23.8 63.4 %collective-permute-start.276 = (bf16[2,512,256]{2,1,0:T(8,128)(2,1)}, bf16[2,512,256]{2,1,0:T(8,128)(2,1)S(1)}, u32[]{:S(2)}, u32[]{:S(2)}) collective-permute-start(bf16[2,512,256]{2,1,0:T(8,128)(2,1)} %get-tuple-element.2318), channel_id=1, source_target_pairs={{0,8},{8,0},{16,24},{24,16},{1,9},{9,1},{17,25},{25,17},{2,10},{10... | collective-permute-start | bytes 1572872 | tf_op jit(solution)/shard_map/ppermute | solution.py:14
  24.6 62.6 %collective-permute-start.277 = (bf16[2,512,256]{2,1,0:T(8,128)(2,1)}, bf16[2,512,256]{2,1,0:T(8,128)(2,1)S(1)}, u32[]{:S(2)}, u32[]{:S(2)}) collective-permute-start(bf16[2,512,256]{2,1,0:T(8,128)(2,1)} %get-tuple-element.2317), channel_id=1, source_target_pairs={{0,16},{8,24},{16,0},{24,8},{1,17},{9,25},{17,1},{25,9},{2,18},{10... | collective-permute-start | bytes 1572872 | tf_op jit(solution)/shard_map/ppermute | solution.py:14
  27.8 59.5 %collective-permute-start.278 = (bf16[2,512,256]{2,1,0:T(8,128)(2,1)}, bf16[2,512,256]{2,1,0:T(8,128)(2,1)S(1)}, u32[]{:S(2)}, u32[]{:S(2)}) collective-permute-start(bf16[2,512,256]{2,1,0:T(8,128)(2,1)} %get-tuple-element.2316), channel_id=1, source_target_pairs={{0,24},{8,16},{16,8},{24,0},{1,25},{9,17},{17,9},{25,1},{2,26},{10... | collective-permute-start | bytes 1572872 | tf_op jit(solution)/shard_map/ppermute | solution.py:14
  39.6 5.4 %collective-permute-start.263 = (bf16[2,2,128,256]{3,2,1,0:T(8,128)(2,1)S(1)}, bf16[2,2,128,256]{3,2,1,0:T(8,128)(2,1)}, u32[]{:S(2)}, u32[]{:S(2)}) collective-permute-start(bf16[2,2,128,256]{3,2,1,0:T(8,128)(2,1)S(1)} %pad_maximum_fusion.2), channel_id=1, source_target_pairs={{0,1},{1,0},{2,3},{3,2},{4,5},{5,4},{6,7},{7,6},{8,9},{9,8},{10,11... | collective-permute-start | bytes 786440 | tf_op jit(solution)/shard_map/cond/branch_1_fun/ppermute | solution.py:14
  73.3 7.6 %collective-permute-start.265 = (f32[2,16,2048]{2,1,0:T(8,128)S(1)}, f32[2,16,2048]{2,1,0:T(8,128)S(1)}, u32[]{:S(2)}, u32[]{:S(2)}) collective-permute-start(f32[2,16,2048]{2,1,0:T(8,128)S(1)} %dynamic-slice_bitcast_fusion.3), channel_id=1, source_target_pairs={{0,2},{1,3},{2,0},{3,1},{4,6},{5,7},{6,4},{7,5},{8,10},{9,11},{10,... | collective-permute-start | bytes 786440 | tf_op jit(solution)/shard_map/cond/branch_1_fun/ppermute | solution.py:14
  75.1 7.6 %collective-permute-start.268 = (f32[2,16,2048]{2,1,0:T(8,128)S(1)}, f32[2,16,2048]{2,1,0:T(8,128)S(1)}, u32[]{:S(2)}, u32[]{:S(2)}) collective-permute-start(f32[2,16,2048]{2,1,0:T(8,128)S(1)} %dynamic-slice_bitcast_fusion.2), channel_id=1, source_target_pairs={{0,4},{1,5},{2,6},{3,7},{4,0},{5,1},{6,2},{7,3},{8,12},{9,13},{10,... | collective-permute-start | bytes 786440 | tf_op jit(solution)/shard_map/cond/branch_1_fun/ppermute | solution.py:14
  87.2 5.8 %collective-permute-start.279 = (bf16[2,16,2048]{2,1,0:T(8,128)(2,1)S(1)}, bf16[2,16,2048]{2,1,0:T(8,128)(2,1)S(1)}, u32[]{:S(2)}, u32[]{:S(2)}) collective-permute-start(bf16[2,16,2048]{2,1,0:T(8,128)(2,1)S(1)} %get-tuple-element.2347), channel_id=1, source_target_pairs={{0,24},{8,16},{16,8},{24,0},{1,25},{9,17},{17,9},{25,1},{2,26},{10... | collective-permute-start | bytes 393224 | tf_op jit(solution)/shard_map/ppermute | solution.py:14
  90.2 10.1 %collective-permute-start.280 = (bf16[2,16,2048]{2,1,0:T(8,128)(2,1)S(1)}, bf16[2,16,2048]{2,1,0:T(8,128)(2,1)S(1)}, u32[]{:S(2)}, u32[]{:S(2)}) collective-permute-start(bf16[2,16,2048]{2,1,0:T(8,128)(2,1)S(1)} %get-tuple-element.2347), channel_id=1, source_target_pairs={{0,16},{8,24},{16,0},{24,8},{1,17},{9,25},{17,1},{25,9},{2,18},{10... | collective-permute-start | bytes 393224 | tf_op jit(solution)/shard_map/ppermute | solution.py:14
  90.2 10.1 %collective-permute-start.281 = (bf16[2,16,2048]{2,1,0:T(8,128)(2,1)S(1)}, bf16[2,16,2048]{2,1,0:T(8,128)(2,1)S(1)}, u32[]{:S(2)}, u32[]{:S(2)}) collective-permute-start(bf16[2,16,2048]{2,1,0:T(8,128)(2,1)S(1)} %get-tuple-element.2347), channel_id=1, source_target_pairs={{0,8},{8,0},{16,24},{24,16},{1,9},{9,1},{17,25},{25,17},{2,10},{10... | collective-permute-start | bytes 393224 | tf_op jit(solution)/shard_map/ppermute | solution.py:14
  104.0 42.5 %collective-permute-start.282 = (bf16[2,512,256]{2,1,0:T(8,128)(2,1)}, bf16[2,512,256]{2,1,0:T(8,128)(2,1)}, u32[]{:S(2)}, u32[]{:S(2)}) collective-permute-start(bf16[2,512,256]{2,1,0:T(8,128)(2,1)} %get-tuple-element.2314), channel_id=1, source_target_pairs={{0,8},{8,0},{16,24},{24,16},{1,9},{9,1},{17,25},{25,17},{2,10},{10... | collective-permute-start | bytes 1572872 | tf_op jit(solution)/shard_map/ppermute | solution.py:14
  104.0 42.5 %collective-permute-start.283 = (bf16[2,512,256]{2,1,0:T(8,128)(2,1)}, bf16[2,512,256]{2,1,0:T(8,128)(2,1)}, u32[]{:S(2)}, u32[]{:S(2)}) collective-permute-start(bf16[2,512,256]{2,1,0:T(8,128)(2,1)} %get-tuple-element.2313), channel_id=1, source_target_pairs={{0,16},{8,24},{16,0},{24,8},{1,17},{9,25},{17,1},{25,9},{2,18},{10... | collective-permute-start | bytes 1572872 | tf_op jit(solution)/shard_map/ppermute | solution.py:14
  105.8 40.7 %collective-permute-start.284 = (bf16[2,512,256]{2,1,0:T(8,128)(2,1)}, bf16[2,512,256]{2,1,0:T(8,128)(2,1)S(1)}, u32[]{:S(2)}, u32[]{:S(2)}) collective-permute-start(bf16[2,512,256]{2,1,0:T(8,128)(2,1)} %get-tuple-element.2312), channel_id=1, source_target_pairs={{0,24},{8,16},{16,8},{24,0},{1,25},{9,17},{17,9},{25,1},{2,26},{10... | collective-permute-start | bytes 1572872 | tf_op jit(solution)/shard_map/ppermute | solution.py:14
  113.3 5.7 %collective-permute-start = (bf16[4,16,2048]{2,1,0:T(8,128)(2,1)S(1)}, bf16[4,16,2048]{2,1,0:T(8,128)(2,1)S(1)}, u32[]{:S(2)}, u32[]{:S(2)}) collective-permute-start(bf16[4,16,2048]{2,1,0:T(8,128)(2,1)S(1)} %get-tuple-element.1606), channel_id=1, source_target_pairs={{0,2},{1,3},{2,0},{3,1},{4,6},{5,7},{6,4},{7,5},{8,10},{9,11},{10,... | collective-permute-start | bytes 786440 | tf_op jit(solution)/shard_map/cond/branch_1_fun/ppermute | solution.py:14
  113.7 5.9 %collective-permute-start.3 = (bf16[4,16,2048]{2,1,0:T(8,128)(2,1)S(1)}, bf16[4,16,2048]{2,1,0:T(8,128)(2,1)}, u32[]{:S(2)}, u32[]{:S(2)}) collective-permute-start(bf16[4,16,2048]{2,1,0:T(8,128)(2,1)S(1)} %get-tuple-element.1607), channel_id=1, source_target_pairs={{0,4},{1,5},{2,6},{3,7},{4,0},{5,1},{6,2},{7,3},{8,12},{9,13},{10,... | collective-permute-start | bytes 786440 | tf_op jit(solution)/shard_map/cond/branch_1_fun/ppermute | solution.py:14
  121.0 10.2 %collective-permute-start.1 = (bf16[2,4,16,2048]{3,2,1,0:T(8,128)(2,1)S(1)}, bf16[2,4,16,2048]{3,2,1,0:T(8,128)(2,1)S(1)}, u32[]{:S(2)}, u32[]{:S(2)}) collective-permute-start(bf16[2,4,16,2048]{3,2,1,0:T(8,128)(2,1)S(1)} %pad_maximum_fusion.10), channel_id=1, source_target_pairs={{0,4},{1,5},{2,6},{3,7},{4,0},{5,1},{6,2},{7,3},{8,12},{9,13},{10,... | collective-permute-start | bytes 1572872 | tf_op jit(solution)/shard_map/cond/branch_1_fun/ppermute | solution.py:14
  121.3 9.9 %collective-permute-start.4 = (bf16[2,4,16,2048]{3,2,1,0:T(8,128)(2,1)S(1)}, bf16[2,4,16,2048]{3,2,1,0:T(8,128)(2,1)S(1)}, u32[]{:S(2)}, u32[]{:S(2)}) collective-permute-start(bf16[2,4,16,2048]{3,2,1,0:T(8,128)(2,1)S(1)} %pad_maximum_fusion.11), channel_id=1, source_target_pairs={{0,2},{1,3},{2,0},{3,1},{4,6},{5,7},{6,4},{7,5},{8,10},{9,11},{10,... | collective-permute-start | bytes 1572872 | tf_op jit(solution)/shard_map/cond/branch_1_fun/ppermute | solution.py:14
  132.7 7.1 %collective-permute-start.2 = (bf16[2,2,4,16,2048]{4,3,2,1,0:T(8,128)(2,1)}, bf16[2,2,4,16,2048]{4,3,2,1,0:T(8,128)(2,1)}, u32[]{:S(2)}, u32[]{:S(2)}) collective-permute-start(bf16[2,2,4,16,2048]{4,3,2,1,0:T(8,128)(2,1)} %pad_maximum_fusion.8), channel_id=1, source_target_pairs={{0,1},{1,0},{2,3},{3,2},{4,5},{5,4},{6,7},{7,6},{8,9},{9,8},{10,11... | collective-permute-start | bytes 3145736 | tf_op jit(solution)/shard_map/cond/branch_1_fun/ppermute | solution.py:14
  181.1 15.0 %collective-permute-start.154 = (f32[352,384]{1,0:T(8,128)}, f32[352,384]{1,0:T(8,128)}, u32[]{:S(2)}, u32[]{:S(2)}) collective-permute-start(f32[352,384]{1,0:T(8,128)} %fusion.1071), channel_id=1, source_target_pairs={{0,8},{24,16},{1,9},{25,17},{2,10},{26,18},{3,11},{27,19},{4,12},{... | collective-permute-start | bytes 1622024 | tf_op jit(solution)/shard_map/cond/branch_4_fun/ppermute | solution.py:140
  190.2 18.3 %collective-permute-start.150 = (f32[352,384]{1,0:T(8,128)}, f32[352,384]{1,0:T(8,128)}, u32[]{:S(2)}, u32[]{:S(2)}) collective-permute-start(f32[352,384]{1,0:T(8,128)} %fusion.1079), channel_id=1, source_target_pairs={{0,8},{24,16},{1,9},{25,17},{2,10},{26,18},{3,11},{27,19},{4,12},{... | collective-permute-start | bytes 1622024 | tf_op jit(solution)/shard_map/cond/branch_4_fun/ppermute | solution.py:140
  199.4 28.1 %collective-permute-start.156 = (f32[352,384]{1,0:T(8,128)}, f32[352,384]{1,0:T(8,128)}, u32[]{:S(2)}, u32[]{:S(2)}) collective-permute-start(f32[352,384]{1,0:T(8,128)} %add.7260), channel_id=1, source_target_pairs={{8,16},{16,8},{9,17},{17,9},{10,18},{18,10},{11,19},{19,11},{12,20... | collective-permute-start | bytes 1622024 | tf_op jit(solution)/shard_map/cond/branch_4_fun/ppermute | solution.py:142
  203.1 24.4 %collective-permute-start.155 = (f32[352,384]{1,0:T(8,128)}, f32[352,384]{1,0:T(8,128)}, u32[]{:S(2)}, u32[]{:S(2)}) collective-permute-start(f32[352,384]{1,0:T(8,128)} %fusion.1069), channel_id=1, source_target_pairs={{0,8},{24,16},{1,9},{25,17},{2,10},{26,18},{3,11},{27,19},{4,12},{... | collective-permute-start | bytes 1622024 | tf_op jit(solution)/shard_map/cond/branch_4_fun/ppermute | solution.py:140
  211.7 17.5 %collective-permute-start.152 = (f32[352,384]{1,0:T(8,128)}, f32[352,384]{1,0:T(8,128)}, u32[]{:S(2)}, u32[]{:S(2)}) collective-permute-start(f32[352,384]{1,0:T(8,128)} %add.7254), channel_id=1, source_target_pairs={{8,16},{16,8},{9,17},{17,9},{10,18},{18,10},{11,19},{19,11},{12,20... | collective-permute-start | bytes 1622024 | tf_op jit(solution)/shard_map/cond/branch_4_fun/ppermute | solution.py:142
  215.5 14.8 %collective-permute-start.151 = (f32[352,384]{1,0:T(8,128)}, f32[352,384]{1,0:T(8,128)}, u32[]{:S(2)}, u32[]{:S(2)}) collective-permute-start(f32[352,384]{1,0:T(8,128)} %fusion.1077), channel_id=1, source_target_pairs={{0,8},{24,16},{1,9},{25,17},{2,10},{26,18},{3,11},{27,19},{4,12},{... | collective-permute-start | bytes 1622024 | tf_op jit(solution)/shard_map/cond/branch_4_fun/ppermute | solution.py:140
  229.1 12.6 %collective-permute-start.157 = (f32[352,384]{1,0:T(8,128)S(1)}, f32[352,384]{1,0:T(8,128)S(1)}, u32[]{:S(2)}, u32[]{:S(2)}) collective-permute-start(f32[352,384]{1,0:T(8,128)S(1)} %convolution_add_fusion.187), channel_id=1, source_target_pairs={{0,8},{24,16},{8,0},{16,24},{1,9},{25,17},{9,1},{17,25},{2,10},{26... | collective-permute-start | bytes 1622024 | tf_op jit(solution)/shard_map/cond/branch_4_fun/ppermute | solution.py:140
  231.7 21.6 %collective-permute-start.153 = (f32[352,384]{1,0:T(8,128)S(1)}, f32[352,384]{1,0:T(8,128)S(1)}, u32[]{:S(2)}, u32[]{:S(2)}) collective-permute-start(f32[352,384]{1,0:T(8,128)S(1)} %convolution_add_fusion.189), channel_id=1, source_target_pairs={{0,8},{24,16},{8,0},{16,24},{1,9},{25,17},{9,1},{17,25},{2,10},{26... | collective-permute-start | bytes 1622024 | tf_op jit(solution)/shard_map/cond/branch_4_fun/ppermute | solution.py:140
  236.6 16.7 %collective-permute-start.172 = (f32[352,384]{1,0:T(8,128)S(1)}, f32[352,384]{1,0:T(8,128)S(1)}, u32[]{:S(2)}, u32[]{:S(2)}) collective-permute-start(f32[352,384]{1,0:T(8,128)S(1)} %add.7319), channel_id=1, source_target_pairs={{8,16},{16,8},{9,17},{17,9},{10,18},{18,10},{11,19},{19,11},{12,20... | collective-permute-start | bytes 1622024 | tf_op jit(solution)/shard_map/cond/branch_4_fun/ppermute | solution.py:142
  240.0 26.4 %collective-permute-start.158 = (f32[352,384]{1,0:T(8,128)S(1)}, f32[352,384]{1,0:T(8,128)S(1)}, u32[]{:S(2)}, u32[]{:S(2)}) collective-permute-start(f32[352,384]{1,0:T(8,128)S(1)} %add.7263), channel_id=1, source_target_pairs={{8,16},{16,8},{9,17},{17,9},{10,18},{18,10},{11,19},{19,11},{12,20... | collective-permute-start | bytes 1622024 | tf_op jit(solution)/shard_map/cond/branch_4_fun/ppermute | solution.py:142
  255.5 27.0 %collective-permute-start.174 = (f32[352,384]{1,0:T(8,128)}, f32[352,384]{1,0:T(8,128)}, u32[]{:S(2)}, u32[]{:S(2)}) collective-permute-start(f32[352,384]{1,0:T(8,128)} %add.7322), channel_id=1, source_target_pairs={{8,16},{16,8},{9,17},{17,9},{10,18},{18,10},{11,19},{19,11},{12,20... | collective-permute-start | bytes 1622024 | tf_op jit(solution)/shard_map/cond/branch_4_fun/ppermute | solution.py:142
  259.3 23.3 %collective-permute-start.173 = (f32[352,384]{1,0:T(8,128)}, f32[352,384]{1,0:T(8,128)}, u32[]{:S(2)}, u32[]{:S(2)}) collective-permute-start(f32[352,384]{1,0:T(8,128)} %convolution_add_fusion.171), channel_id=1, source_target_pairs={{0,8},{24,16},{8,0},{16,24},{1,9},{25,17},{9,1},{17,25},{2,10},{26... | collective-permute-start | bytes 1622024 | tf_op jit(solution)/shard_map/cond/branch_4_fun/ppermute | solution.py:140
  268.6 21.6 %collective-permute-start.160 = (f32[352,384]{1,0:T(8,128)}, f32[352,384]{1,0:T(8,128)}, u32[]{:S(2)}, u32[]{:S(2)}) collective-permute-start(f32[352,384]{1,0:T(8,128)} %add.7271), channel_id=1, source_target_pairs={{8,16},{16,8},{9,17},{17,9},{10,18},{18,10},{11,19},{19,11},{12,20... | collective-permute-start | bytes 1622024 | tf_op jit(solution)/shard_map/cond/branch_4_fun/ppermute | solution.py:142
  272.4 17.8 %collective-permute-start.159 = (f32[352,384]{1,0:T(8,128)}, f32[352,384]{1,0:T(8,128)}, u32[]{:S(2)}, u32[]{:S(2)}) collective-permute-start(f32[352,384]{1,0:T(8,128)} %convolution_add_fusion.186), channel_id=1, source_target_pairs={{0,8},{24,16},{8,0},{16,24},{1,9},{25,17},{9,1},{17,25},{2,10},{26... | collective-permute-start | bytes 1622024 | tf_op jit(solution)/shard_map/cond/branch_4_fun/ppermute | solution.py:140
  285.0 15.6 %collective-permute-start.176 = (f32[352,384]{1,0:T(8,128)S(1)}, f32[352,384]{1,0:T(8,128)S(1)}, u32[]{:S(2)}, u32[]{:S(2)}) collective-permute-start(f32[352,384]{1,0:T(8,128)S(1)} %add.7325), channel_id=1, source_target_pairs={{8,16},{16,8},{9,17},{17,9},{10,18},{18,10},{11,19},{19,11},{12,20... | collective-permute-start | bytes 1622024 | tf_op jit(solution)/shard_map/cond/branch_4_fun/ppermute | solution.py:142
  287.6 13.0 %collective-permute-start.175 = (f32[352,384]{1,0:T(8,128)S(1)}, f32[352,384]{1,0:T(8,128)S(1)}, u32[]{:S(2)}, u32[]{:S(2)}) collective-permute-start(f32[352,384]{1,0:T(8,128)S(1)} %convolution_add_fusion.169), channel_id=1, source_target_pairs={{0,8},{24,16},{8,0},{16,24},{1,9},{25,17},{9,1},{17,25},{2,10},{26... | collective-permute-start | bytes 1622024 | tf_op jit(solution)/shard_map/cond/branch_4_fun/ppermute | solution.py:140
  292.7 9.5 %collective-permute-start.162 = (f32[352,384]{1,0:T(8,128)S(1)}, f32[352,384]{1,0:T(8,128)S(1)}, u32[]{:S(2)}, u32[]{:S(2)}) collective-permute-start(f32[352,384]{1,0:T(8,128)S(1)} %add.7279), channel_id=1, source_target_pairs={{8,16},{16,8},{9,17},{17,9},{10,18},{18,10},{11,19},{19,11},{12,20... | collective-permute-start | bytes 1622024 | tf_op jit(solution)/shard_map/cond/branch_4_fun/ppermute | solution.py:142
  294.9 15.3 %collective-permute-start.161 = (f32[352,384]{1,0:T(8,128)S(1)}, f32[352,384]{1,0:T(8,128)S(1)}, u32[]{:S(2)}, u32[]{:S(2)}) collective-permute-start(f32[352,384]{1,0:T(8,128)S(1)} %convolution_add_fusion.184), channel_id=1, source_target_pairs={{0,8},{24,16},{8,0},{16,24},{1,9},{25,17},{9,1},{17,25},{2,10},{26... | collective-permute-start | bytes 1622024 | tf_op jit(solution)/shard_map/cond/branch_4_fun/ppermute | solution.py:140
  302.1 19.9 %collective-permute-start.177 = (f32[352,384]{1,0:T(8,128)S(1)}, f32[352,384]{1,0:T(8,128)S(1)}, u32[]{:S(2)}, u32[]{:S(2)}) collective-permute-start(f32[352,384]{1,0:T(8,128)S(1)} %convolution_add_fusion.167), channel_id=1, source_target_pairs={{0,8},{24,16},{8,0},{16,24},{1,9},{25,17},{9,1},{17,25},{2,10},{26... | collective-permute-start | bytes 1622024 | tf_op jit(solution)/shard_map/cond/branch_4_fun/ppermute | solution.py:140
  311.7 10.4 %collective-permute-start.178 = (f32[352,384]{1,0:T(8,128)S(1)}, f32[352,384]{1,0:T(8,128)S(1)}, u32[]{:S(2)}, u32[]{:S(2)}) collective-permute-start(f32[352,384]{1,0:T(8,128)S(1)} %add.7328), channel_id=1, source_target_pairs={{8,16},{16,8},{9,17},{17,9},{10,18},{18,10},{11,19},{19,11},{12,20... | collective-permute-start | bytes 1622024 | tf_op jit(solution)/shard_map/cond/branch_4_fun/ppermute | solution.py:142
  315.2 18.1 %collective-permute-start.163 = (f32[352,384]{1,0:T(8,128)S(1)}, f32[352,384]{1,0:T(8,128)S(1)}, u32[]{:S(2)}, u32[]{:S(2)}) collective-permute-start(f32[352,384]{1,0:T(8,128)S(1)} %convolution_add_fusion.182), channel_id=1, source_target_pairs={{0,8},{24,16},{8,0},{16,24},{1,9},{25,17},{9,1},{17,25},{2,10},{26... | collective-permute-start | bytes 1622024 | tf_op jit(solution)/shard_map/cond/branch_4_fun/ppermute | solution.py:140
  318.4 14.9 %collective-permute-start.164 = (f32[352,384]{1,0:T(8,128)S(1)}, f32[352,384]{1,0:T(8,128)S(1)}, u32[]{:S(2)}, u32[]{:S(2)}) collective-permute-start(f32[352,384]{1,0:T(8,128)S(1)} %add.7287), channel_id=1, source_target_pairs={{8,16},{16,8},{9,17},{17,9},{10,18},{18,10},{11,19},{19,11},{12,20... | collective-permute-start | bytes 1622024 | tf_op jit(solution)/shard_map/cond/branch_4_fun/ppermute | solution.py:142
  323.4 21.0 %collective-permute-start.180 = (f32[352,384]{1,0:T(8,128)S(1)}, f32[352,384]{1,0:T(8,128)S(1)}, u32[]{:S(2)}, u32[]{:S(2)}) collective-permute-start(f32[352,384]{1,0:T(8,128)S(1)} %add.7331), channel_id=1, source_target_pairs={{8,16},{16,8},{9,17},{17,9},{10,18},{18,10},{11,19},{19,11},{12,20... | collective-permute-start | bytes 1622024 | tf_op jit(solution)/shard_map/cond/branch_4_fun/ppermute | solution.py:142
  325.6 18.8 %collective-permute-start.179 = (f32[352,384]{1,0:T(8,128)S(1)}, f32[352,384]{1,0:T(8,128)S(1)}, u32[]{:S(2)}, u32[]{:S(2)}) collective-permute-start(f32[352,384]{1,0:T(8,128)S(1)} %convolution_add_fusion.165), channel_id=1, source_target_pairs={{0,8},{24,16},{8,0},{16,24},{1,9},{25,17},{9,1},{17,25},{2,10},{26... | collective-permute-start | bytes 1622024 | tf_op jit(solution)/shard_map/cond/branch_4_fun/ppermute | solution.py:140
  334.7 9.7 %collective-permute-start.166 = (f32[352,384]{1,0:T(8,128)S(1)}, f32[352,384]{1,0:T(8,128)S(1)}, u32[]{:S(2)}, u32[]{:S(2)}) collective-permute-start(f32[352,384]{1,0:T(8,128)S(1)} %add.7295), channel_id=1, source_target_pairs={{8,16},{16,8},{9,17},{17,9},{10,18},{18,10},{11,19},{19,11},{12,20... | collective-permute-start | bytes 1622024 | tf_op jit(solution)/shard_map/cond/branch_4_fun/ppermute | solution.py:142
  337.0 14.3 %collective-permute-start.165 = (f32[352,384]{1,0:T(8,128)S(1)}, f32[352,384]{1,0:T(8,128)S(1)}, u32[]{:S(2)}, u32[]{:S(2)}) collective-permute-start(f32[352,384]{1,0:T(8,128)S(1)} %convolution_add_fusion.180), channel_id=1, source_target_pairs={{0,8},{24,16},{8,0},{16,24},{1,9},{25,17},{9,1},{17,25},{2,10},{26... | collective-permute-start | bytes 1622024 | tf_op jit(solution)/shard_map/cond/branch_4_fun/ppermute | solution.py:140
  352.7 12.9 %collective-permute-start.167 = (f32[352,384]{1,0:T(8,128)S(1)}, f32[352,384]{1,0:T(8,128)S(1)}, u32[]{:S(2)}, u32[]{:S(2)}) collective-permute-start(f32[352,384]{1,0:T(8,128)S(1)} %convolution_add_fusion.178), channel_id=1, source_target_pairs={{0,8},{24,16},{8,0},{16,24},{1,9},{25,17},{9,1},{17,25},{2,10},{26... | collective-permute-start | bytes 1622024 | tf_op jit(solution)/shard_map/cond/branch_4_fun/ppermute | solution.py:140
  356.7 8.9 %collective-permute-start.168 = (f32[352,384]{1,0:T(8,128)S(1)}, f32[352,384]{1,0:T(8,128)S(1)}, u32[]{:S(2)}, u32[]{:S(2)}) collective-permute-start(f32[352,384]{1,0:T(8,128)S(1)} %add.7303), channel_id=1, source_target_pairs={{8,16},{16,8},{9,17},{17,9},{10,18},{18,10},{11,19},{19,11},{12,20... | collective-permute-start | bytes 1622024 | tf_op jit(solution)/shard_map/cond/branch_4_fun/ppermute | solution.py:142
  360.2 13.4 %collective-permute-start.181 = (f32[352,384]{1,0:T(8,128)S(1)}, f32[352,384]{1,0:T(8,128)S(1)}, u32[]{:S(2)}, u32[]{:S(2)}) collective-permute-start(f32[352,384]{1,0:T(8,128)S(1)} %convolution_add_fusion.163), channel_id=1, source_target_pairs={{0,8},{24,16},{8,0},{16,24},{1,9},{25,17},{9,1},{17,25},{2,10},{26... | collective-permute-start | bytes 1622024 | tf_op jit(solution)/shard_map/cond/branch_4_fun/ppermute | solution.py:140
  362.0 11.6 %collective-permute-start.182 = (f32[352,384]{1,0:T(8,128)S(1)}, f32[352,384]{1,0:T(8,128)S(1)}, u32[]{:S(2)}, u32[]{:S(2)}) collective-permute-start(f32[352,384]{1,0:T(8,128)S(1)} %add.7334), channel_id=1, source_target_pairs={{8,16},{16,8},{9,17},{17,9},{10,18},{18,10},{11,19},{19,11},{12,20... | collective-permute-start | bytes 1622024 | tf_op jit(solution)/shard_map/cond/branch_4_fun/ppermute | solution.py:142
  367.1 15.8 %collective-permute-start.170 = (f32[352,384]{1,0:T(8,128)S(1)}, f32[352,384]{1,0:T(8,128)S(1)}, u32[]{:S(2)}, u32[]{:S(2)}) collective-permute-start(f32[352,384]{1,0:T(8,128)S(1)} %add.7311), channel_id=1, source_target_pairs={{8,16},{16,8},{9,17},{17,9},{10,18},{18,10},{11,19},{19,11},{12,20... | collective-permute-start | bytes 1622024 | tf_op jit(solution)/shard_map/cond/branch_4_fun/ppermute | solution.py:142
  369.2 20.3 %collective-permute-start.169 = (f32[352,384]{1,0:T(8,128)S(1)}, f32[352,384]{1,0:T(8,128)S(1)}, u32[]{:S(2)}, u32[]{:S(2)}) collective-permute-start(f32[352,384]{1,0:T(8,128)S(1)} %convolution_add_fusion.176), channel_id=1, source_target_pairs={{8,0},{16,24},{9,1},{17,25},{10,2},{18,26},{11,3},{19,27},{12,4},{... | collective-permute-start | bytes 1622024 | tf_op jit(solution)/shard_map/cond/branch_4_fun/ppermute | solution.py:140
  375.1 17.2 %collective-permute-start.184 = (f32[352,384]{1,0:T(8,128)S(1)}, f32[352,384]{1,0:T(8,128)S(1)}, u32[]{:S(2)}, u32[]{:S(2)}) collective-permute-start(f32[352,384]{1,0:T(8,128)S(1)} %add.7337), channel_id=1, source_target_pairs={{8,16},{16,8},{9,17},{17,9},{10,18},{18,10},{11,19},{19,11},{12,20... | collective-permute-start | bytes 1622024 | tf_op jit(solution)/shard_map/cond/branch_4_fun/ppermute | solution.py:142
  377.2 21.5 %collective-permute-start.183 = (f32[352,384]{1,0:T(8,128)S(1)}, f32[352,384]{1,0:T(8,128)S(1)}, u32[]{:S(2)}, u32[]{:S(2)}) collective-permute-start(f32[352,384]{1,0:T(8,128)S(1)} %convolution_add_fusion.161), channel_id=1, source_target_pairs={{8,0},{16,24},{9,1},{17,25},{10,2},{18,26},{11,3},{19,27},{12,4},{... | collective-permute-start | bytes 1622024 | tf_op jit(solution)/shard_map/cond/branch_4_fun/ppermute | solution.py:140
  391.0 17.7 %collective-permute-start.171 = (f32[352,384]{1,0:T(8,128)S(1)}, f32[352,384]{1,0:T(8,128)S(1)}, u32[]{:S(2)}, u32[]{:S(2)}) collective-permute-start(f32[352,384]{1,0:T(8,128)S(1)} %convolution_add_fusion.174), channel_id=1, source_target_pairs={{8,0},{16,24},{9,1},{17,25},{10,2},{18,26},{11,3},{19,27},{12,4},{... | collective-permute-start | bytes 1622024 | tf_op jit(solution)/shard_map/cond/branch_4_fun/ppermute | solution.py:140
  400.2 20.0 %collective-permute-start.185 = (f32[352,384]{1,0:T(8,128)S(1)}, f32[352,384]{1,0:T(8,128)S(1)}, u32[]{:S(2)}, u32[]{:S(2)}) collective-permute-start(f32[352,384]{1,0:T(8,128)S(1)} %convolution_add_fusion.159), channel_id=1, source_target_pairs={{8,0},{16,24},{9,1},{17,25},{10,2},{18,26},{11,3},{19,27},{12,4},{... | collective-permute-start | bytes 1622024 | tf_op jit(solution)/shard_map/cond/branch_4_fun/ppermute | solution.py:140
  432.8 4.3 collective-permute-start.285
  437.4 20.3 %collective-permute-start.288 = (f32[4,3,2,128]{3,2,0,1:T(2,128)S(1)}, f32[4,3,2,128]{3,2,0,1:T(2,128)S(1)}, u32[]{:S(2)}, u32[]{:S(2)}) collective-permute-start(f32[4,3,2,128]{3,2,0,1:T(2,128)S(1)} %pad_maximum_fusion.27), channel_id=1, source_target_pairs={{0,6},{1,7},{2,4},{3,5},{4,2},{5,3},{6,0},{7,1},{8,14},{9,15},{10,... | collective-permute-start | bytes 36872 | tf_op jit(solution)/shard_map/ppermute | solution.py:14
  437.7 21.1 %collective-permute-start.290 = (f32[4,3,2,128]{3,2,0,1:T(2,128)S(1)}, f32[4,3,2,128]{3,2,0,1:T(2,128)S(1)}, u32[]{:S(2)}, u32[]{:S(2)}) collective-permute-start(f32[4,3,2,128]{3,2,0,1:T(2,128)S(1)} %pad_maximum_fusion.27), channel_id=1, source_target_pairs={{0,4},{1,5},{2,6},{3,7},{4,0},{5,1},{6,2},{7,3},{8,12},{9,13},{10,... | collective-permute-start | bytes 36872 | tf_op jit(solution)/shard_map/ppermute | solution.py:14
  439.0 19.8 %collective-permute-start.292 = (f32[4,3,2,128]{3,2,0,1:T(2,128)S(1)}, f32[4,3,2,128]{3,2,0,1:T(2,128)S(1)}, u32[]{:S(2)}, u32[]{:S(2)}) collective-permute-start(f32[4,3,2,128]{3,2,0,1:T(2,128)S(1)} %pad_maximum_fusion.27), channel_id=1, source_target_pairs={{0,2},{1,3},{2,0},{3,1},{4,6},{5,7},{6,4},{7,5},{8,10},{9,11},{10,... | collective-permute-start | bytes 36872 | tf_op jit(solution)/shard_map/ppermute | solution.py:14
  440.1 21.0 %collective-permute-start.294 = (f32[4,3,2,128]{3,2,0,1:T(2,128)S(1)}, f32[4,3,2,128]{3,2,0,1:T(2,128)S(1)}, u32[]{:S(2)}, u32[]{:S(2)}) collective-permute-start(f32[4,3,2,128]{3,2,0,1:T(2,128)S(1)} %pad_maximum_fusion.27), channel_id=1, source_target_pairs={{0,1},{1,0},{2,3},{3,2},{4,5},{5,4},{6,7},{7,6},{8,9},{9,8},{10,11... | collective-permute-start | bytes 36872 | tf_op jit(solution)/shard_map/ppermute | solution.py:14
  (32 other events, 468.2 us)
